TPU v7x, 32 devices: a whole 2x2x4 slice. The times are simulated.
32 devices in a mesh: dp: 4 (over z), expert: 8 (over y, x, core).
Axes of the slice: x: 2, y: 2, z: 4, core: 2. Of those that a mesh axis runs over, the one named last changes fastest.
Arguments:
- tokens: bfloat16 [2, 6144, 1024], P(None, ('dp', 'expert')), may hold values from -6 to 6
- cotangent: bfloat16 [2, 6144, 1024], P(None, ('dp', 'expert')), may hold values from -6 to 6
- lengths: int32 [2, 32], P(None, ('dp', 'expert')), may hold values from 1 to 192, as said below
- routes: int32 [2, 6144, 16], P(None, ('dp', 'expert')), may hold values from 0 to 95, all different within a row; in each aligned block of 192 rows (0 to 191, 192 to 383, ..., all dimensions but the last counted through in order) at most 40 rows name the same one
- head_choice: int32 [2, 6144, 4, 2], P(None, ('dp', 'expert')), may hold values from 0 to 4, all different within a row
- placement: int32 [96], replicated, may hold values from 0 to 95, each once
- gain_master: float32 [1024], P(('dp', 'expert')), may hold values from 0.5 to 1.5
- gain_moment: float32 [1024], P(('dp', 'expert')), may hold values from -640 to 640
- gain_average: float32 [1024], P(('dp', 'expert')), may hold values from 0.5 to 1.5
- qkv_master: float32 [1024, 3584], P(('dp', 'expert')), may hold values from -0.1875 to 0.1875
- qkv_moment: float32 [1024, 3584], P(('dp', 'expert')), may hold values from -640 to 640
- qkv_average: float32 [1024, 3584], P(('dp', 'expert')), may hold values from -0.1875 to 0.1875
- select_master: float32 [1024, 40], P(('dp', 'expert')), may hold values from -0.125 to 0.125
- select_moment: float32 [1024, 40], P(('dp', 'expert')), may hold values from -2048 to 2048
- select_average: float32 [1024, 40], P(('dp', 'expert')), may hold values from -0.125 to 0.125
- router_master: float32 [1024, 96], P(('dp', 'expert')), may hold values from -0.0625 to 0.0625
- router_moment: float32 [1024, 96], P(('dp', 'expert')), may hold values from -512 to 512
- router_average: float32 [1024, 96], P(('dp', 'expert')), may hold values from -0.0625 to 0.0625
- heads_out_master: float32 [2560, 1024], P(('dp', 'expert')), may hold values from -3 to 3
- heads_out_moment: float32 [2560, 1024], P(('dp', 'expert')), may hold values from -64 to 64
- heads_out_average: float32 [2560, 1024], P(('dp', 'expert')), may hold values from -3 to 3
- up_master: float32 [96, 1024, 128], P('expert', 'dp'), may hold values from -0.1875 to 0.1875
- up_moment: float32 [96, 1024, 128], P('expert', 'dp'), may hold values from -128 to 128
- up_average: float32 [96, 1024, 128], P('expert', 'dp'), may hold values from -0.1875 to 0.1875
- down_master: float32 [96, 1024, 128], P('expert', 'dp'), may hold values from -0.25 to 0.25
- down_moment: float32 [96, 1024, 128], P('expert', 'dp'), may hold values from -112 to 112
- down_average: float32 [96, 1024, 128], P('expert', 'dp'), may hold values from -0.25 to 0.25
Outputs:
- mixed: bfloat16 [2, 6144, 1024], P(None, ('dp', 'expert'))
- grad_input: float32 [2, 6144, 1024], P(None, ('dp', 'expert'))
- gain_moment_new: float32 [1024], P(('dp', 'expert'))
- gain_average_new: float32 [1024], P(('dp', 'expert'))
- gain_new: float32 [1024], P(('dp', 'expert'))
- gain_new_low: bfloat16 [1024], P(('dp', 'expert'))
- qkv_moment_new: float32 [1024, 3584], P(('dp', 'expert'))
- qkv_average_new: float32 [1024, 3584], P(('dp', 'expert'))
- qkv_new: float32 [1024, 3584], P(('dp', 'expert'))
- qkv_new_low: bfloat16 [1024, 3584], P(('dp', 'expert'))
- select_moment_new: float32 [1024, 40], P(('dp', 'expert'))
- select_average_new: float32 [1024, 40], P(('dp', 'expert'))
- select_new: float32 [1024, 40], P(('dp', 'expert'))
- select_new_low: bfloat16 [1024, 40], P(('dp', 'expert'))
- router_moment_new: float32 [1024, 96], P(('dp', 'expert'))
- router_average_new: float32 [1024, 96], P(('dp', 'expert'))
- router_new: float32 [1024, 96], P(('dp', 'expert'))
- router_new_low: bfloat16 [1024, 96], P(('dp', 'expert'))
- heads_out_moment_new: float32 [2560, 1024], P(('dp', 'expert'))
- heads_out_average_new: float32 [2560, 1024], P(('dp', 'expert'))
- heads_out_new: float32 [2560, 1024], P(('dp', 'expert'))
- heads_out_new_low: bfloat16 [2560, 1024], P(('dp', 'expert'))
- up_moment_new: float32 [96, 1024, 128], P('expert', 'dp')
- up_average_new: float32 [96, 1024, 128], P('expert', 'dp')
- up_new: float32 [96, 1024, 128], P('expert', 'dp')
- up_new_low: bfloat16 [96, 1024, 128], P('expert', 'dp')
- down_moment_new: float32 [96, 1024, 128], P('expert', 'dp')
- down_average_new: float32 [96, 1024, 128], P('expert', 'dp')
- down_new: float32 [96, 1024, 128], P('expert', 'dp')
- down_new_low: bfloat16 [96, 1024, 128], P('expert', 'dp')
Inputs may be any that keep to these rules, and one draw needn't show every extreme that they name: `lengths`: in each micro-batch some sequence slot has all 192 rows live. `routes`: each row names 16 different experts; in each micro-batch no expert is named by more than 40 rows of one sequence slot, a bound that some block reaches. `head_choice`: each head of each row names 2 different experts. A permutation: expert r uses the weights of slot placement[r].
All inputs are finite; a program needn't handle non-finite values.
Results may differ from a plain program's by a relative error of at most 0.015.
The roundings to bfloat16 on the way count: a program that leaves them out, or rounds other values in their place, can miss the bound.
Values may be sent and summed in bfloat16 or wider, within the bound.
A program may use at most 256 MiB of HBM per device.

v0:
```python
import math

import jax
import jax.numpy as jnp
from jax import lax
from jax.sharding import PartitionSpec as P

D = 1024
H = 4
HD = 128
NV = 5
F = 128
TOPK = 16
MB = 2


momentum_decay = 0.9
average_decay = 0.5
rate_factor = 0.4
epsilon = 1e-05


def layer_normed(inputs, gain_row):
    centred = inputs - jnp.mean(inputs, axis=-1, keepdims=True)
    variance = jnp.mean(centred * centred, axis=-1, keepdims=True)
    return centred * lax.rsqrt(variance + epsilon) * gain_row


def picked_mask(picks, number):
    return jnp.sum(
        (picks[..., None] == jnp.arange(number, dtype=jnp.int32)).astype(jnp.float32), axis=-2
    )


def step_rates(total_tokens, experts):
    root_tokens = math.sqrt(total_tokens)
    expert_share = math.sqrt(TOPK / experts)
    spread_list = (
        0.3,
        D ** (-0.5),
        (2 * D) ** (-0.5),
        (9 * D) ** (-0.5),
        0.5,
        D ** (-0.5),
        (4 * F) ** (-0.5),
    )
    gradient_list = (1.0, 1.0, 3.0, 2.0 * expert_share, 0.1, 0.5 * expert_share, 0.4 * expert_share)
    return tuple(
        (
            rate_factor * spread_value / (gradient_value * root_tokens)
            for spread_value, gradient_value in zip(spread_list, gradient_list)
        )
    )


def update_weight(master, moment, average, gradient, step_size):
    new_moment = momentum_decay * moment + gradient
    new_weight = master - step_size * (gradient + momentum_decay * new_moment)
    new_average = average_decay * average + (1.0 - average_decay) * new_weight
    return (new_moment, new_average, new_weight, new_weight.astype(jnp.bfloat16))


def head_gates(select, value_mask, out_mask):
    row_count = value_mask.shape[0]
    value_gate = jax.nn.sigmoid(select[:, : H * NV]).reshape(row_count, H, NV) * value_mask
    out_gate = jax.nn.sigmoid(select[:, H * NV :]).reshape(row_count, H, NV) * out_mask
    return (value_gate, out_gate)


def slot_positions(route_rows, placement, experts, most):
    pair_count = route_rows.shape[0] * route_rows.shape[1]
    flat_slots = placement[route_rows].reshape(-1)
    pair_order = jnp.argsort(flat_slots, stable=True)
    sorted_slots = flat_slots[pair_order]
    starts = jnp.searchsorted(sorted_slots, jnp.arange(experts, dtype=jnp.int32))
    sorted_ranks = jnp.arange(pair_count, dtype=jnp.int32) - starts[sorted_slots]
    slot_ranks = jnp.zeros((pair_count,), jnp.int32).at[pair_order].set(sorted_ranks)
    return flat_slots * most + slot_ranks


def masked_scores(queries, keys_all, length):
    position = jnp.arange(queries.shape[0], dtype=jnp.int32)
    scores = jnp.einsum(
        "ihd,jhd->hij", queries, keys_all, preferred_element_type=jnp.float32
    ) * HD ** (-0.5)
    allowed = (position[None, :] <= position[:, None]) & (position[None, :] < length)
    return jnp.where(allowed[None], scores, -1e30)


def fetch_dense(gain_low, qkv_low, select_low, router_low, heads_low):
    return (
        lax.all_gather(gain_low, ("dp", "expert"), axis=0, tiled=True),
        lax.all_gather(qkv_low, ("dp", "expert"), axis=0, tiled=True),
        lax.all_gather(select_low, ("dp", "expert"), axis=0, tiled=True),
        lax.all_gather(router_low, ("dp", "expert"), axis=0, tiled=True),
        lax.all_gather(heads_low, ("dp", "expert"), axis=0, tiled=True),
    )


def fetch_experts(up_low, down_low):
    return (
        lax.all_gather(up_low, "dp", axis=1, tiled=True),
        lax.all_gather(down_low, "dp", axis=1, tiled=True),
    )


def reduce_dense(grad_gain, grad_qkv, grad_select, grad_router, grad_heads):
    return (
        lax.psum_scatter(grad_gain, ("dp", "expert"), scatter_dimension=0, tiled=True),
        lax.psum_scatter(grad_qkv, ("dp", "expert"), scatter_dimension=0, tiled=True),
        lax.psum_scatter(grad_select, ("dp", "expert"), scatter_dimension=0, tiled=True),
        lax.psum_scatter(grad_router, ("dp", "expert"), scatter_dimension=0, tiled=True),
        lax.psum_scatter(grad_heads, ("dp", "expert"), scatter_dimension=0, tiled=True),
    )


def reduce_experts(grad_up, grad_down):
    return (
        lax.psum_scatter(
            grad_up.astype(jnp.bfloat16), "dp", scatter_dimension=1, tiled=True
        ).astype(jnp.float32),
        lax.psum_scatter(
            grad_down.astype(jnp.bfloat16), "dp", scatter_dimension=1, tiled=True
        ).astype(jnp.float32),
    )


def micro_step(
    tokens, cotangent, length, route_rows, pick_rows, placement, dense, experts_full, axis_count
):
    gain_low, qkv_low, select_low, router_low, heads_low = dense
    up_full, down_full = experts_full
    rows_here = tokens.shape[0]
    experts = placement.shape[0]
    exp_dev = up_full.shape[0]
    most = (5 * rows_here * TOPK + 4 * experts - 1) // (4 * experts)
    split = 2 * H * HD
    pair_count = rows_here * TOPK
    tokens_float = tokens.astype(jnp.float32)
    live_rows = (jnp.arange(rows_here, dtype=jnp.int32) < length).astype(jnp.float32)
    value_mask = picked_mask(pick_rows, NV)
    out_mask = value_mask * live_rows[:, None, None]
    normed, norm_back = jax.vjp(layer_normed, tokens_float, gain_low.astype(jnp.float32))
    normed_low = normed.astype(jnp.bfloat16)
    query_key = jnp.dot(normed_low, qkv_low[:, :split], preferred_element_type=jnp.float32).astype(
        jnp.bfloat16
    )
    values_all = jnp.dot(tokens, qkv_low[:, split:], preferred_element_type=jnp.float32)
    select = jnp.dot(tokens, select_low, preferred_element_type=jnp.float32)
    (value_gate, out_gate), gate_back = jax.vjp(
        lambda logits_in: head_gates(logits_in, value_mask, out_mask), select
    )
    values_split = values_all.reshape(rows_here, H, NV, HD)
    values_low = jnp.sum(value_gate[..., None] * values_split, axis=2).astype(jnp.bfloat16)
    queries = query_key[:, : H * HD].reshape(rows_here, H, HD)
    keys_all = query_key[:, H * HD :].reshape(rows_here, H, HD)
    masked = masked_scores(queries, keys_all, length)
    top_score = jnp.max(masked, axis=-1, keepdims=True)
    expo = jnp.exp(masked - top_score)
    expo_sum = jnp.sum(expo, axis=-1, keepdims=True)
    log_total = top_score + jnp.log(expo_sum)
    attention_low = (expo / expo_sum).astype(jnp.bfloat16)
    attended = jnp.einsum(
        "hij,jhd->ihd", attention_low, values_low, preferred_element_type=jnp.float32
    )
    mixed_heads = (
        (out_gate[..., None] * attended[:, :, None, :])
        .reshape(rows_here, H * NV * HD)
        .astype(jnp.bfloat16)
    )
    middle = tokens_float + jnp.dot(mixed_heads, heads_low, preferred_element_type=jnp.float32)
    middle_low = middle.astype(jnp.bfloat16)
    logits = jnp.dot(middle_low, router_low, preferred_element_type=jnp.float32)
    sig_chosen = jax.nn.sigmoid(jnp.take_along_axis(logits, route_rows, axis=1))
    gate_values = sig_chosen * live_rows[:, None]
    destination = slot_positions(route_rows, placement, experts, most)
    pair_token = jnp.arange(pair_count, dtype=jnp.int32) // TOPK
    send = jnp.zeros((experts * most, D), jnp.bfloat16).at[destination].set(middle_low[pair_token])
    received = lax.all_to_all(
        send.reshape(axis_count, exp_dev * most, D),
        "expert",
        split_axis=0,
        concat_axis=0,
        tiled=True,
    )
    received = received.reshape(axis_count, exp_dev, most, D)
    pre_act = jnp.einsum("secd,edf->secf", received, up_full, preferred_element_type=jnp.float32)
    hidden_float, gelu_back = jax.vjp(jax.nn.gelu, pre_act)
    hidden = hidden_float.astype(jnp.bfloat16)
    result = jnp.einsum(
        "secf,edf->secd", hidden, down_full, preferred_element_type=jnp.float32
    ).astype(jnp.bfloat16)
    returned = lax.all_to_all(
        result.reshape(axis_count, exp_dev * most, D),
        "expert",
        split_axis=0,
        concat_axis=0,
        tiled=True,
    )
    pair_out = returned.reshape(experts * most, D)[destination].reshape(rows_here, TOPK, D)
    moe_sum = jnp.sum(gate_values[..., None] * pair_out, axis=1)
    mixed = (middle + moe_sum).astype(jnp.bfloat16)
    grad_out = cotangent.astype(jnp.float32)
    d_gate = jnp.einsum("rkd,rd->rk", pair_out, cotangent, preferred_element_type=jnp.float32)
    d_pair = (
        (gate_values[..., None] * grad_out[:, None, :]).astype(jnp.bfloat16).reshape(pair_count, D)
    )
    d_send = jnp.zeros((experts * most, D), jnp.bfloat16).at[destination].set(d_pair)
    d_result = lax.all_to_all(
        d_send.reshape(axis_count, exp_dev * most, D),
        "expert",
        split_axis=0,
        concat_axis=0,
        tiled=True,
    )
    d_result = d_result.reshape(axis_count, exp_dev, most, D)
    d_hidden = jnp.einsum("secd,edf->secf", d_result, down_full, preferred_element_type=jnp.float32)
    d_pre = gelu_back(d_hidden)[0].astype(jnp.bfloat16)
    grad_down = jnp.einsum("secd,secf->edf", d_result, hidden, preferred_element_type=jnp.float32)
    grad_up = jnp.einsum("secd,secf->edf", received, d_pre, preferred_element_type=jnp.float32)
    d_rows = jnp.einsum(
        "secf,edf->secd", d_pre, up_full, preferred_element_type=jnp.float32
    ).astype(jnp.bfloat16)
    rows_back = lax.all_to_all(
        d_rows.reshape(axis_count, exp_dev * most, D),
        "expert",
        split_axis=0,
        concat_axis=0,
        tiled=True,
    )
    rows_back = rows_back.reshape(experts * most, D)[destination].reshape(rows_here, TOPK, D)
    d_from_rows = jnp.sum(rows_back, axis=1, dtype=jnp.float32)
    d_chosen = d_gate * live_rows[:, None] * sig_chosen * (1.0 - sig_chosen)
    expert_ids = jnp.arange(experts, dtype=jnp.int32)
    d_logits = jnp.sum(
        (route_rows[..., None] == expert_ids).astype(jnp.float32) * d_chosen[..., None], axis=1
    ).astype(jnp.bfloat16)
    grad_router = jnp.einsum("rd,re->de", middle_low, d_logits, preferred_element_type=jnp.float32)
    d_middle = (
        grad_out
        + d_from_rows
        + jnp.einsum("re,de->rd", d_logits, router_low, preferred_element_type=jnp.float32)
    )
    d_branch = d_middle.astype(jnp.bfloat16)
    grad_heads = jnp.einsum("rv,rd->vd", mixed_heads, d_branch, preferred_element_type=jnp.float32)
    d_mixed = jnp.einsum(
        "rd,vd->rv", d_branch, heads_low, preferred_element_type=jnp.float32
    ).reshape(rows_here, H, NV, HD)
    d_attended = jnp.sum(out_gate[..., None] * d_mixed, axis=2).astype(jnp.bfloat16)
    d_out_gate = jnp.sum(d_mixed * attended[:, :, None, :], axis=-1)
    attention = jnp.exp(masked_scores(queries, keys_all, length) - log_total)
    attention_again = attention.astype(jnp.bfloat16)
    d_attention = jnp.einsum(
        "ihd,jhd->hij", d_attended, values_low, preferred_element_type=jnp.float32
    )
    d_scores = (
        attention * (d_attention - jnp.sum(attention * d_attention, axis=-1, keepdims=True))
    ).astype(jnp.bfloat16)
    d_values = jnp.einsum(
        "hij,ihd->jhd", attention_again, d_attended, preferred_element_type=jnp.float32
    ).astype(jnp.bfloat16)
    d_queries = jnp.einsum(
        "hij,jhd->ihd", d_scores, keys_all, preferred_element_type=jnp.float32
    ) * HD ** (-0.5)
    d_keys = jnp.einsum(
        "hij,ihd->jhd", d_scores, queries, preferred_element_type=jnp.float32
    ) * HD ** (-0.5)
    d_query_key = jnp.concatenate(
        [d_queries.reshape(rows_here, H * HD), d_keys.reshape(rows_here, H * HD)], axis=1
    ).astype(jnp.bfloat16)
    d_value_gate = jnp.sum(d_values[:, :, None, :] * values_split, axis=-1)
    d_values_all = (
        (value_gate[..., None] * d_values[:, :, None, :])
        .reshape(rows_here, H * NV * HD)
        .astype(jnp.bfloat16)
    )
    d_select = gate_back((d_value_gate, d_out_gate))[0].astype(jnp.bfloat16)
    grad_qkv = jnp.concatenate(
        [
            jnp.einsum("rd,rq->dq", normed_low, d_query_key, preferred_element_type=jnp.float32),
            jnp.einsum("rd,rv->dv", tokens, d_values_all, preferred_element_type=jnp.float32),
        ],
        axis=1,
    )
    grad_select = jnp.einsum("rd,rs->ds", tokens, d_select, preferred_element_type=jnp.float32)
    d_normed = jnp.einsum(
        "rq,dq->rd", d_query_key, qkv_low[:, :split], preferred_element_type=jnp.float32
    )
    d_tokens_norm, grad_gain = norm_back(d_normed)
    d_tokens = (
        d_middle
        + d_tokens_norm
        + jnp.einsum(
            "rv,dv->rd", d_values_all, qkv_low[:, split:], preferred_element_type=jnp.float32
        )
        + jnp.einsum("rs,ds->rd", d_select, select_low, preferred_element_type=jnp.float32)
    )
    return (
        mixed,
        d_tokens,
        (grad_gain, grad_qkv, grad_select, grad_router, grad_heads),
        (grad_up, grad_down),
    )


def body(
    tokens,
    cotangent,
    lengths,
    routes,
    head_choice,
    placement,
    gain_master,
    gain_moment,
    gain_average,
    qkv_master,
    qkv_moment,
    qkv_average,
    select_master,
    select_moment,
    select_average,
    router_master,
    router_moment,
    router_average,
    heads_out_master,
    heads_out_moment,
    heads_out_average,
    up_master,
    up_moment,
    up_average,
    down_master,
    down_moment,
    down_average,
):
    dense_low = (
        gain_master.astype(jnp.bfloat16),
        qkv_master.astype(jnp.bfloat16),
        select_master.astype(jnp.bfloat16),
        router_master.astype(jnp.bfloat16),
        heads_out_master.astype(jnp.bfloat16),
    )
    expert_low = (up_master.astype(jnp.bfloat16), down_master.astype(jnp.bfloat16))
    axis_count = lax.axis_size("expert")
    dense_total = None
    expert_total = None
    mixed_parts = []
    input_parts = []
    for micro_index in range(MB):
        dense_now = fetch_dense(*dense_low)
        expert_now = fetch_experts(*expert_low)
        mixed, d_tokens, dense_grads, expert_grads = micro_step(
            tokens[micro_index],
            cotangent[micro_index],
            lengths[micro_index, 0],
            routes[micro_index],
            head_choice[micro_index],
            placement,
            dense_now,
            expert_now,
            axis_count,
        )
        mixed_parts.append(mixed)
        input_parts.append(d_tokens)
        dense_grads = reduce_dense(*dense_grads)
        expert_grads = reduce_experts(*expert_grads)
        if dense_total is None:
            dense_total = dense_grads
            expert_total = expert_grads
        else:
            dense_total = tuple(
                (
                    first_term + second_term
                    for first_term, second_term in zip(dense_total, dense_grads)
                )
            )
            expert_total = tuple(
                (
                    first_term + second_term
                    for first_term, second_term in zip(expert_total, expert_grads)
                )
            )
    step_sizes = step_rates(
        MB * tokens.shape[1] * lax.axis_size("dp") * axis_count, placement.shape[0]
    )
    gain_out = update_weight(gain_master, gain_moment, gain_average, dense_total[0], step_sizes[0])
    qkv_out = update_weight(qkv_master, qkv_moment, qkv_average, dense_total[1], step_sizes[1])
    select_out = update_weight(
        select_master, select_moment, select_average, dense_total[2], step_sizes[2]
    )
    router_out = update_weight(
        router_master, router_moment, router_average, dense_total[3], step_sizes[3]
    )
    heads_out_out = update_weight(
        heads_out_master, heads_out_moment, heads_out_average, dense_total[4], step_sizes[4]
    )
    up_out = update_weight(up_master, up_moment, up_average, expert_total[0], step_sizes[5])
    down_out = update_weight(down_master, down_moment, down_average, expert_total[1], step_sizes[6])
    return (
        jnp.stack(mixed_parts),
        jnp.stack(input_parts),
        gain_out[0],
        gain_out[1],
        gain_out[2],
        gain_out[3],
        qkv_out[0],
        qkv_out[1],
        qkv_out[2],
        qkv_out[3],
        select_out[0],
        select_out[1],
        select_out[2],
        select_out[3],
        router_out[0],
        router_out[1],
        router_out[2],
        router_out[3],
        heads_out_out[0],
        heads_out_out[1],
        heads_out_out[2],
        heads_out_out[3],
        up_out[0],
        up_out[1],
        up_out[2],
        up_out[3],
        down_out[0],
        down_out[1],
        down_out[2],
        down_out[3],
    )


def solution(mesh):
    in_specs = (
        P(None, ("dp", "expert"), None),
        P(None, ("dp", "expert"), None),
        P(None, ("dp", "expert")),
        P(None, ("dp", "expert"), None),
        P(None, ("dp", "expert"), None, None),
        P(),
        P(("dp", "expert")),
        P(("dp", "expert")),
        P(("dp", "expert")),
        P(("dp", "expert"), None),
        P(("dp", "expert"), None),
        P(("dp", "expert"), None),
        P(("dp", "expert"), None),
        P(("dp", "expert"), None),
        P(("dp", "expert"), None),
        P(("dp", "expert"), None),
        P(("dp", "expert"), None),
        P(("dp", "expert"), None),
        P(("dp", "expert"), None),
        P(("dp", "expert"), None),
        P(("dp", "expert"), None),
        P("expert", "dp", None),
        P("expert", "dp", None),
        P("expert", "dp", None),
        P("expert", "dp", None),
        P("expert", "dp", None),
        P("expert", "dp", None),
    )
    out_specs = (
        P(None, ("dp", "expert"), None),
        P(None, ("dp", "expert"), None),
        P(("dp", "expert")),
        P(("dp", "expert")),
        P(("dp", "expert")),
        P(("dp", "expert")),
        P(("dp", "expert"), None),
        P(("dp", "expert"), None),
        P(("dp", "expert"), None),
        P(("dp", "expert"), None),
        P(("dp", "expert"), None),
        P(("dp", "expert"), None),
        P(("dp", "expert"), None),
        P(("dp", "expert"), None),
        P(("dp", "expert"), None),
        P(("dp", "expert"), None),
        P(("dp", "expert"), None),
        P(("dp", "expert"), None),
        P(("dp", "expert"), None),
        P(("dp", "expert"), None),
        P(("dp", "expert"), None),
        P(("dp", "expert"), None),
        P("expert", "dp", None),
        P("expert", "dp", None),
        P("expert", "dp", None),
        P("expert", "dp", None),
        P("expert", "dp", None),
        P("expert", "dp", None),
        P("expert", "dp", None),
        P("expert", "dp", None),
    )
    return jax.shard_map(body, mesh=mesh, in_specs=in_specs, out_specs=out_specs, check_vma=False)
```

profile of v0, /device:TPU:0, one launch (start us, length us, event | category | flops | bytes accessed | tf_op | source)
XLA Modules:
  0.0 1927.4 jit_solution(7307053655528072652)
XLA Ops:
  12.7 18.7 gather_fusion.6
  37.2 17.4 gather_fusion.7
  69.4 18.7 gather_fusion.2
  93.8 17.4 gather_fusion.3
  126.2 42.5 %all-reduce.4 = bf16[1024]{0:T(1024)(128)(2,1)S(1)} all-reduce(bf16[1024]{0:T(1024)(128)(2,1)S(1)} %dynamic-update-slice), channel_id=1, replica_groups=mesh['dp'=4,'expert'=8] {'dp','expert'}, use_global_device_ids=true, to_apply=%add.4 | all-reduce | flops 1024 | bytes 4096
  168.9 40.9 %all_gather.28 = bf16[1024,40]{1,0:T(8,128)(2,1)S(1)} all-gather(bf16[32,40]{1,0:T(8,128)(2,1)S(1)} %convert_element_type.334), channel_id=1, replica_groups=mesh['dp'=4,'expert'=8] {'dp','expert'}, dimensions={0}, use_global_device_ids=true | all-gather | bytes 84480 | tf_op jit(solution)/shard_map/all_gather | solution.py:94
  211.5 18.7 gather_fusion.8
  242.1 18.7 gather_fusion.4
  272.5 37.8 %all_gather.32 = bf16[1024,96]{1,0:T(8,128)(2,1)S(1)} all-gather(bf16[32,96]{1,0:T(8,128)(2,1)S(1)} %convert_element_type.348), channel_id=1, replica_groups=mesh['dp'=4,'expert'=8] {'dp','expert'}, dimensions={0}, use_global_device_ids=true | all-gather | bytes 202752 | tf_op jit(solution)/shard_map/all_gather | solution.py:95
  341.6 19.3 %gather_fusion.12 = f32[3072]{0:T(1024)S(1)} fusion(f32[192,96]{1,0:T(8,128)S(1)} %fusion.257, s32[3072]{0:T(1024)S(1)} %reshape.825), kind=kCustom, calls=%fused_computation.clone | custom fusion | bytes 49152 | tf_op jit(solution)/shard_map/jit(take_along_axis)/gather | solution.py:174
  364.5 19.7 %scatter_custom_fusion.4 = bf16[3840,1024]{1,0:T(8,128)(2,1)} fusion(s32[3072]{0:T(1024)S(1)} %get-tuple-element.465, bf16[3072,1024]{1,0:T(8,128)(2,1)} %fusion.9, bf16[]{:T(256)} %constant.131.clone.1), kind=kCustom, calls=%fused_computation.77 | custom fusion | bytes 7864832 | tf_op jit(solution)/shard_map/scatter | solution.py:208
  389.2 50.5 %scatter_custom_fusion.1 = bf16[3840,1024]{1,0:T(8,128)(2,1)} fusion(s32[3072]{0:T(1024)S(1)} %get-tuple-element.465, bf16[192,1024]{1,0:T(8,128)(2,1)} %copy-done.46, s32[3072]{0:T(1024)S(1)} %broadcast_clamp_fusion.2, bf16[]{:T(256)} %constant.131.clone.1), kind=kCustom, calls=%fused_computation.68 | custom fusion | bytes 7864832 | tf_op jit(solution)/shard_map/scatter | solution.py:178
  439.7 37.9 %all-to-all-done.4 = bf16[8,480,1024]{2,1,0:T(8,128)(2,1)} async-done(((bf16[8,480,1024]{2,1,0:T(8,128)(2,1)}), bf16[8,480,1024]{2,1,0:T(8,128)(2,1)}, u32[]{:S(2)}, u32[]{:S(2)}) %all-to-all-start.4) | async-done | bytes 7864352 | tf_op jit(solution)/shard_map/all_to_all | solution.py:209
  500.0 41.3 %scatter_custom_fusion.3 = bf16[3840,1024]{1,0:T(8,128)(2,1)} fusion(s32[3072]{0:T(1024)S(1)} %get-tuple-element.396, bf16[192,1024]{1,0:T(8,128)(2,1)S(1)} %get-tuple-element.445, s32[3072]{0:T(1024)S(1)} %broadcast_clamp_fusion.2, bf16[]{:T(256)} %constant.131.clone.1), kind=kCustom, calls=%fused_computation.66 | custom fusion | bytes 7864322 | tf_op jit(solution)/shard_map/scatter | solution.py:178
  541.3 29.9 %all-to-all-done = bf16[8,480,1024]{2,1,0:T(8,128)(2,1)} async-done(((bf16[8,480,1024]{2,1,0:T(8,128)(2,1)}), bf16[8,480,1024]{2,1,0:T(8,128)(2,1)}, u32[]{:S(2)}, u32[]{:S(2)}) %all-to-all-start) | async-done | bytes 7864352 | tf_op jit(solution)/shard_map/all_to_all | solution.py:179
  577.7 19.3 %gather_fusion.13 = f32[3072]{0:T(1024)S(1)} fusion(f32[192,96]{1,0:T(8,128)S(1)} %fusion.258, s32[3072]{0:T(1024)S(1)} %reshape.830), kind=kCustom, calls=%fused_computation.3.clone | custom fusion | bytes 49152 | tf_op jit(solution)/shard_map/jit(take_along_axis)/gather | solution.py:174
  600.7 19.4 %scatter_custom_fusion.5 = bf16[3840,1024]{1,0:T(8,128)(2,1)} fusion(s32[3072]{0:T(1024)S(1)} %get-tuple-element.396, bf16[3072,1024]{1,0:T(8,128)(2,1)} %fusion.8, bf16[]{:T(256)} %constant.131.clone.1), kind=kCustom, calls=%fused_computation.75 | custom fusion | bytes 7864832 | tf_op jit(solution)/shard_map/scatter | solution.py:208
  620.2 44.5 %all-to-all-done.2 = bf16[8,480,1024]{2,1,0:T(8,128)(2,1)} async-done(((bf16[8,480,1024]{2,1,0:T(8,128)(2,1)}), bf16[8,480,1024]{2,1,0:T(8,128)(2,1)}, u32[]{:S(2)}, u32[]{:S(2)}) %all-to-all-start.2) | async-done | bytes 7864352 | tf_op jit(solution)/shard_map/all_to_all | solution.py:179
  696.3 61.8 %all-to-all-done.6 = bf16[8,480,1024]{2,1,0:T(8,128)(2,1)} async-done(((bf16[8,480,1024]{2,1,0:T(8,128)(2,1)}), bf16[8,480,1024]{2,1,0:T(8,128)(2,1)}, u32[]{:S(2)}, u32[]{:S(2)}) %all-to-all-start.6) | async-done | bytes 7864352 | tf_op jit(solution)/shard_map/all_to_all | solution.py:209
  766.4 56.4 %reduce-scatter.19.cloned.1.call-done = bf16[12,256,128]{2,1,0:T(8,128)(2,1)} async-done(((bf16[12,1024,128]{2,1,0:T(8,128)(2,1)}), bf16[12,256,128]{2,1,0:T(8,128)(2,1)}) %reduce-scatter.19.cloned.1.call-update) | async-done | bytes 786448 | tf_op jit(solution)/shard_map/reduce_scatter | solution.py:122
  827.0 63.3 %all-gather.11.cloned.1.call-done = bf16[12,1024,128]{2,1,0:T(8,128)(2,1)} async-done(((bf16[12,256,128]{2,1,0:T(8,128)(2,1)}), bf16[12,1024,128]{2,1,0:T(8,128)(2,1)}) %all-gather.11.cloned.1.call-update) | async-done | bytes 3145744 | tf_op jit(solution)/shard_map/all_gather | solution.py:103
  925.2 74.2 %all-to-all-done.5 = bf16[8,480,1024]{2,1,0:T(8,128)(2,1)} async-done(((bf16[8,480,1024]{2,1,0:T(8,128)(2,1)}), bf16[8,480,1024]{2,1,0:T(8,128)(2,1)}, u32[]{:S(2)}, u32[]{:S(2)}) %all-to-all-start.5) | async-done | bytes 7864352 | tf_op jit(solution)/shard_map/all_to_all | solution.py:224
  1012.7 80.3 %all-to-all-done.7 = bf16[8,480,1024]{2,1,0:T(8,128)(2,1)} async-done(((bf16[8,480,1024]{2,1,0:T(8,128)(2,1)}), bf16[8,480,1024]{2,1,0:T(8,128)(2,1)}, u32[]{:S(2)}, u32[]{:S(2)}) %all-to-all-start.7) | async-done | bytes 7864352 | tf_op jit(solution)/shard_map/all_to_all | solution.py:224
  1115.3 71.1 %all-to-all-done.3 = bf16[8,480,1024]{2,1,0:T(8,128)(2,1)} async-done(((bf16[8,480,1024]{2,1,0:T(8,128)(2,1)}), bf16[8,480,1024]{2,1,0:T(8,128)(2,1)}, u32[]{:S(2)}, u32[]{:S(2)}) %all-to-all-start.3) | async-done | bytes 7864352 | tf_op jit(solution)/shard_map/all_to_all | solution.py:193
  1201.3 20.6 %gather_fusion.11 = bf16[3072,1024]{1,0:T(8,128)(2,1)} fusion(bf16[3840,1024]{1,0:T(8,128)(2,1)} %bitcast.74, s32[3072]{0:T(1024)S(1)} %copy-done.114), kind=kCustom, calls=%fused_computation.15 | custom fusion | bytes 12595200 | tf_op jit(solution)/shard_map/gather | solution.py:231
  1221.8 20.2 %gather_fusion.9 = bf16[3072,1024]{1,0:T(8,128)(2,1)} fusion(bf16[3840,1024]{1,0:T(8,128)(2,1)} %bitcast.46, s32[3072]{0:T(1024)S(1)} %copy-done.114), kind=kCustom, calls=%fused_computation.13 | custom fusion | bytes 12595200 | tf_op jit(solution)/shard_map/gather | solution.py:200
  1262.9 20.3 %gather_fusion.10 = bf16[3072,1024]{1,0:T(8,128)(2,1)} fusion(bf16[3840,1024]{1,0:T(8,128)(2,1)} %bitcast.56, s32[3072]{0:T(1024)S(1)} %copy-done.113), kind=kCustom, calls=%fused_computation.14 | custom fusion | bytes 12595200 | tf_op jit(solution)/shard_map/gather | solution.py:231
  1283.2 20.2 %gather_fusion.5 = bf16[3072,1024]{1,0:T(8,128)(2,1)} fusion(bf16[3840,1024]{1,0:T(8,128)(2,1)} %bitcast.24, s32[3072]{0:T(1024)S(1)} %copy-done.113), kind=kCustom, calls=%fused_computation.8 | custom fusion | bytes 12595200 | tf_op jit(solution)/shard_map/gather | solution.py:200
  1416.3 39.6 %all-reduce.5 = f32[1024]{0:T(1024)S(1)} all-reduce(f32[1024]{0:T(1024)S(1)} %add.421), channel_id=7, replica_groups=mesh['dp'=4,'expert'=8] {'dp','expert'}, use_global_device_ids=true, to_apply=%region_43.45.clone | all-reduce | flops 1024 | bytes 8192
  1480.8 125.3 %reduce-scatter.21.cloned.1.call-done = f32[32,96]{1,0:T(8,128)} async-done(((f32[1024,96]{1,0:T(8,128)}), f32[32,96]{1,0:T(8,128)}) %reduce-scatter.21.cloned.1.call-update) | async-done | bytes 12304 | tf_op jit(solution)/shard_map/reduce_scatter | solution.py:112
  1608.0 148.9 %reduce-scatter.23.cloned.1.call-done = f32[80,1024]{1,0:T(8,128)} async-done(((f32[2560,1024]{1,0:T(8,128)}), f32[80,1024]{1,0:T(8,128)}) %reduce-scatter.23.cloned.1.call-update) | async-done | bytes 327696 | tf_op jit(solution)/shard_map/reduce_scatter | solution.py:113
  1759.6 157.3 %reduce-scatter.25.cloned.1.call-done = f32[32,3584]{1,0:T(8,128)} async-done(((f32[1024,3584]{1,0:T(8,128)}), f32[32,3584]{1,0:T(8,128)}) %reduce-scatter.25.cloned.1.call-update) | async-done | bytes 458768 | tf_op jit(solution)/shard_map/reduce_scatter | solution.py:110
  (678 shorter events, 464.9 us)
Async XLA Ops:
  8.1 306.3 %all-gather.5.cloned.1.call-start = ((), (), s32[]{:S(2)}) async-start(), calls=%async_computation.16 | async-start | bytes 7569408 | tf_op jit(solution)/shard_map/all_gather | solution.py:93
  9.9 325.6 %all-gather.7.cloned.1.call-start = ((), (), s32[]{:S(2)}) async-start(), calls=%async_computation.17 | async-start | bytes 5406720 | tf_op jit(solution)/shard_map/all_gather | solution.py:96
  12.5 348.6 %copy-start.37 = (s32[1,192,16]{2,1,0:T(8,128)}, s32[1,192,16]{2,1,0:T(8,128)S(1)}, u32[]{:S(2)}) copy-start(s32[1,192,16]{2,1,0:T(8,128)S(1)} %copy.351) | copy-start | bytes 36868
  168.7 315.9 %copy-start.122 = (f32[1024]{0:T(1024)}, f32[1024]{0:T(1024)S(1)}, u32[]{:S(2)}) copy-start(f32[1024]{0:T(1024)S(1)} %convert_element_type.340) | copy-start | bytes 12292
  209.8 273.0 %copy-start.23 = (bf16[1024,40]{1,0:T(8,128)(2,1)}, bf16[1024,40]{1,0:T(8,128)(2,1)S(1)}, u32[]{:S(2)}) copy-start(bf16[1024,40]{1,0:T(8,128)(2,1)S(1)} %all_gather.28) | copy-start | bytes 245764
  384.2 93.4 %all-to-all-start.4 = ((bf16[8,480,1024]{2,1,0:T(8,128)(2,1)}), bf16[8,480,1024]{2,1,0:T(8,128)(2,1)}, u32[]{:S(2)}, u32[]{:S(2)}) async-start(bf16[8,480,1024]{2,1,0:T(8,128)(2,1)} %bitcast.425), calls=%async_computation.4 | async-start | bytes 15728640 | tf_op jit(solution)/shard_map/all_to_all | solution.py:209
  477.6 93.6 %all-to-all-start = ((bf16[8,480,1024]{2,1,0:T(8,128)(2,1)}), bf16[8,480,1024]{2,1,0:T(8,128)(2,1)}, u32[]{:S(2)}, u32[]{:S(2)}) async-start(bf16[8,480,1024]{2,1,0:T(8,128)(2,1)} %bitcast.419), calls=%async_computation | async-start | bytes 15728640 | tf_op jit(solution)/shard_map/all_to_all | solution.py:179
  571.2 93.5 %all-to-all-start.2 = ((bf16[8,480,1024]{2,1,0:T(8,128)(2,1)}), bf16[8,480,1024]{2,1,0:T(8,128)(2,1)}, u32[]{:S(2)}, u32[]{:S(2)}) async-start(bf16[8,480,1024]{2,1,0:T(8,128)(2,1)} %bitcast.420), calls=%async_computation.2 | async-start | bytes 15728640 | tf_op jit(solution)/shard_map/all_to_all | solution.py:179
  576.2 93.7 %all-gather.9.cloned.1.call-start = ((), (), s32[]{:S(2)}) async-start(), calls=%async_computation.18 | async-start | bytes 3932160 | tf_op jit(solution)/shard_map/all_gather | solution.py:102
  664.6 93.4 %all-to-all-start.6 = ((bf16[8,480,1024]{2,1,0:T(8,128)(2,1)}), bf16[8,480,1024]{2,1,0:T(8,128)(2,1)}, u32[]{:S(2)}, u32[]{:S(2)}) async-start(bf16[8,480,1024]{2,1,0:T(8,128)(2,1)} %bitcast.421), calls=%async_computation.6 | async-start | bytes 15728640 | tf_op jit(solution)/shard_map/all_to_all | solution.py:209
  669.6 96.8 %reduce-scatter.17.cloned.1.call-start = ((), (), s32[]{:S(2)}) async-start(), calls=%async_computation.22 | async-start | bytes 3932160 | tf_op jit(solution)/shard_map/reduce_scatter | solution.py:122
  686.6 136.3 %reduce-scatter.19.cloned.1.call-start = ((), (), s32[]{:S(2)}) async-start(), calls=%async_computation.23 | async-start | bytes 3932160 | tf_op jit(solution)/shard_map/reduce_scatter | solution.py:122
  766.1 124.2 %all-gather.11.cloned.1.call-start = ((), (), s32[]{:S(2)}) async-start(), calls=%async_computation.19 | async-start | bytes 3932160 | tf_op jit(solution)/shard_map/all_gather | solution.py:103
  905.4 94.0 %all-to-all-start.5 = ((bf16[8,480,1024]{2,1,0:T(8,128)(2,1)}), bf16[8,480,1024]{2,1,0:T(8,128)(2,1)}, u32[]{:S(2)}, u32[]{:S(2)}) async-start(bf16[8,480,1024]{2,1,0:T(8,128)(2,1)} %bitcast.424), calls=%async_computation.5 | async-start | bytes 15728640 | tf_op jit(solution)/shard_map/all_to_all | solution.py:224
  999.4 93.5 %all-to-all-start.7 = ((bf16[8,480,1024]{2,1,0:T(8,128)(2,1)}), bf16[8,480,1024]{2,1,0:T(8,128)(2,1)}, u32[]{:S(2)}, u32[]{:S(2)}) async-start(bf16[8,480,1024]{2,1,0:T(8,128)(2,1)} %bitcast.423), calls=%async_computation.7 | async-start | bytes 15728640 | tf_op jit(solution)/shard_map/all_to_all | solution.py:224
  1092.9 93.5 %all-to-all-start.3 = ((bf16[8,480,1024]{2,1,0:T(8,128)(2,1)}), bf16[8,480,1024]{2,1,0:T(8,128)(2,1)}, u32[]{:S(2)}, u32[]{:S(2)}) async-start(bf16[8,480,1024]{2,1,0:T(8,128)(2,1)} %bitcast.422), calls=%async_computation.3 | async-start | bytes 15728640 | tf_op jit(solution)/shard_map/all_to_all | solution.py:193
  1098.0 303.3 %reduce-scatter.13.cloned.1.call-start = ((), (), s32[]{:S(2)}) async-start(), calls=%async_computation.20 | async-start | bytes 3932160 | tf_op jit(solution)/shard_map/reduce_scatter | solution.py:119
  1186.5 96.8 %all-to-all-start.1 = ((bf16[8,480,1024]{2,1,0:T(8,128)(2,1)}), bf16[8,480,1024]{2,1,0:T(8,128)(2,1)}, u32[]{:S(2)}, u32[]{:S(2)}) async-start(bf16[8,480,1024]{2,1,0:T(8,128)(2,1)} %bitcast.418), calls=%async_computation.1 | async-start | bytes 15728640 | tf_op jit(solution)/shard_map/all_to_all | solution.py:193
  1191.5 209.8 %reduce-scatter.15.cloned.1.call-start = ((), (), s32[]{:S(2)}) async-start(), calls=%async_computation.21 | async-start | bytes 3932160 | tf_op jit(solution)/shard_map/reduce_scatter | solution.py:119
  1200.6 276.6 %reduce-scatter.27.cloned.1.call-start = ((), (), s32[]{:S(2)}) async-start(), calls=%async_computation.27 | async-start | bytes 540672
  1341.0 265.0 %reduce-scatter.21.cloned.1.call-start = ((), (), s32[]{:S(2)}) async-start(), calls=%async_computation.24 | async-start | bytes 540672 | tf_op jit(solution)/shard_map/reduce_scatter | solution.py:112
  1344.6 412.3 %reduce-scatter.23.cloned.1.call-start = ((), (), s32[]{:S(2)}) async-start(), calls=%async_computation.25 | async-start | bytes 10813440 | tf_op jit(solution)/shard_map/reduce_scatter | solution.py:113
  1354.7 562.2 %reduce-scatter.25.cloned.1.call-start = ((), (), s32[]{:S(2)}) async-start(), calls=%async_computation.26 | async-start | bytes 15138816 | tf_op jit(solution)/shard_map/reduce_scatter | solution.py:110
  1474.5 282.4 %copy-start.48 = (f32[80,1024]{1,0:T(8,128)S(1)}, f32[80,1024]{1,0:T(8,128)}, u32[]{:S(2)}) copy-start(f32[80,1024]{1,0:T(8,128)} %param.51) | copy-start | bytes 983044
  1474.5 282.4 %copy-start.88 = (f32[80,1024]{1,0:T(8,128)S(1)}, f32[80,1024]{1,0:T(8,128)}, u32[]{:S(2)}) copy-start(f32[80,1024]{1,0:T(8,128)} %param.52) | copy-start | bytes 983044
  1474.8 284.0 %copy-start.89 = (f32[80,1024]{1,0:T(8,128)S(1)}, f32[80,1024]{1,0:T(8,128)}, u32[]{:S(2)}) copy-start(f32[80,1024]{1,0:T(8,128)} %param.53) | copy-start | bytes 983044
  1474.8 442.1 %copy-start.42 = (f32[32,3584]{1,0:T(8,128)S(1)}, f32[32,3584]{1,0:T(8,128)}, u32[]{:S(2)}) copy-start(f32[32,3584]{1,0:T(8,128)} %param.42) | copy-start | bytes 1376260
  1474.8 442.1 %copy-start.82 = (f32[32,3584]{1,0:T(8,128)S(1)}, f32[32,3584]{1,0:T(8,128)}, u32[]{:S(2)}) copy-start(f32[32,3584]{1,0:T(8,128)} %param.43) | copy-start | bytes 1376260
  1476.1 442.8 %copy-start.83 = (f32[32,3584]{1,0:T(8,128)S(1)}, f32[32,3584]{1,0:T(8,128)}, u32[]{:S(2)}) copy-start(f32[32,3584]{1,0:T(8,128)} %param.44) | copy-start | bytes 1376260
  1476.7 443.1 %copy-start.153 = (f32[32]{0:T(128)}, f32[32]{0:T(128)S(1)}, u32[]{:S(2)}) copy-start(f32[32]{0:T(128)S(1)} %get-tuple-element.391) | copy-start | bytes 388
  1607.4 312.4 %copy-start.119 = (f32[32,96]{1,0:T(8,128)}, f32[32,96]{1,0:T(8,128)S(1)}, u32[]{:S(2)}) copy-start(f32[32,96]{1,0:T(8,128)S(1)} %get-tuple-element.383) | copy-start | bytes 36868
  1607.4 312.4 %copy-start.1 = (s32[96]{0:T(128)S(1)}, s32[96]{0:T(128)}, u32[]{:S(2)}) copy-start(s32[96]{0:T(128)} %param.38) | copy-start | bytes 1156
  (147 other events, 3038.4 us)
Sparse Core Ops, SparseCore 0:
  12.3 77.6 all-gather.4
  93.5 65.4 all-gather.6
Sparse Core Ops, SparseCore 1:
  578.8 61.9 all-gather.8
  686.7 58.8 reduce-scatter.16
  766.2 56.6 reduce-scatter.18
  827.1 63.2 all-gather.10
  1106.1 59.3 reduce-scatter.12
  1200.7 59.3 reduce-scatter.14
  1341.1 133.2 reduce-scatter.26
  1476.6 129.4 reduce-scatter.20
  1608.2 148.6 reduce-scatter.22
  1759.2 157.6 reduce-scatter.24
where the time goes:
time: 1940 us; the launch traced here: 1930 us
  waiting for transfers between devices  951 us (49%)
  local copies, waits for them, and re-layouts  493 us (25%)
  blocking collectives  161 us (8%)
  matrix products  159 us (8%)
  other arithmetic  103 us (5%)
  starting transfers between devices  41.8 us (2%)
    reduce_scatter x1, waiting for transfers between devices, reduce_dense(): lax.psum_scatter(grad_qkv, ('dp', 'expert'), scatter_dimension=0, tiled=T...  157 us
    all_to_all x2, waiting for transfers between devices, micro_step(): lax.all_to_all(d_rows.reshape(axis_count, exp_dev * most, D), 'expert', s...  155 us
    reduce_scatter x1, waiting for transfers between devices, reduce_dense(): lax.psum_scatter(grad_heads, ('dp', 'expert'), scatter_dimension=0, tiled...  149 us
    reduce_scatter x1, waiting for transfers between devices, reduce_dense(): lax.psum_scatter(grad_router, ('dp', 'expert'), scatter_dimension=0, tile...  125 us
    all_to_all x2, waiting for transfers between devices, micro_step(): lax.all_to_all(d_send.reshape(axis_count, exp_dev * most, D), 'expert', s...  99.7 us
    scatter x2, local copies, waits for them, and re-layouts, micro_step(): jnp.zeros((experts * most, D), jnp.bfloat16).at[destination]  91.8 us
    unnamed x2, blocking collectives  82.2 us
    all_to_all x2, waiting for transfers between devices, micro_step(): lax.all_to_all(send.reshape(axis_count, exp_dev * most, D), 'expert', spl...  74.4 us
  transfers between devices with their start and end apart: 20, of which 12 were waited for; matrix products, arithmetic and copies ran while one was open for 35% of the time, Pallas kernels for 0%

commit v1 on v0

v1 whole, which is shorter than its diff:
```python
import functools
import math

import jax
import jax.numpy as jnp
from jax import lax
from jax.experimental import pallas as pl
from jax.experimental.pallas import tpu as pltpu
from jax.sharding import PartitionSpec as P

D = 1024
H = 4
HD = 128
NV = 5
F = 128
TOPK = 16
MB = 2
QK = 2 * H * HD
VAL = H * NV * HD
SEL = 2 * H * NV

momentum_decay = 0.9
average_decay = 0.5
rate_factor = 0.4
epsilon = 1e-05
BF = jnp.bfloat16
F32 = jnp.float32


def step_rates(total_tokens, experts):
    root_tokens = math.sqrt(total_tokens)
    expert_share = math.sqrt(TOPK / experts)
    spread_list = (
        0.3,
        D ** (-0.5),
        (2 * D) ** (-0.5),
        (9 * D) ** (-0.5),
        0.5,
        D ** (-0.5),
        (4 * F) ** (-0.5),
    )
    gradient_list = (1.0, 1.0, 3.0, 2.0 * expert_share, 0.1, 0.5 * expert_share, 0.4 * expert_share)
    return tuple(
        rate_factor * spread_value / (gradient_value * root_tokens)
        for spread_value, gradient_value in zip(spread_list, gradient_list)
    )


def update_weight(master, moment, average, gradient, step_size):
    new_moment = momentum_decay * moment + gradient
    new_weight = master - step_size * (gradient + momentum_decay * new_moment)
    new_average = average_decay * average + (1.0 - average_decay) * new_weight
    return (new_moment, new_average, new_weight, new_weight.astype(BF))


def dot_nt(a, b):
    return lax.dot_general(a, b, (((1,), (1,)), ((), ())), preferred_element_type=F32)


def dot_tn(a, b):
    return lax.dot_general(a, b, (((0,), (0,)), ((), ())), preferred_element_type=F32)


def dot_nn(a, b):
    return jnp.dot(a, b, preferred_element_type=F32)


MESH = pl.DeviceIdType.MESH


class Place:
    def __init__(self):
        self.z = lax.axis_index("dp")
        self.e = lax.axis_index("expert")
        core = self.e % 2
        x = (self.e // 2) % 2
        y = self.e // 4
        self.sib = self.e + 1 - 2 * core
        self.xnb = self.e + 2 - 4 * x
        self.ynb = self.e + 4 - 8 * y
        self.diag = self.xnb + 4 - 8 * y
        self.core, self.x, self.y = core, x, y


def greet(place, line, owners):
    barrier = pltpu.get_barrier_semaphore()
    z = place.z
    for e in (place.sib, place.xnb, place.ynb):
        pl.semaphore_signal(barrier, inc=1, device_id=(z, e), device_id_type=MESH)
    peers = 3
    if line:

        @pl.when(z > 0)
        def _():
            pl.semaphore_signal(barrier, inc=1, device_id=(z - 1, place.e), device_id_type=MESH)

        @pl.when(z < owners - 1)
        def _():
            pl.semaphore_signal(barrier, inc=1, device_id=(z + 1, place.e), device_id_type=MESH)

        peers = peers + (z + owners - 1) // owners + (2 * owners - 2 - z) // owners
    pl.semaphore_wait(barrier, peers)


XS, YS, FA, FB, S0, S1, S2, S3, UP, DOWN = range(10)

def gather_kernel(owners, group, lines, halves, *refs):
    n = len(lines)
    ins, outs, (send, recv, own) = refs[:n], refs[n : 2 * n], refs[2 * n :]
    place = Place()
    z = place.z
    copies_own = []
    for i in range(n):
        rows = ins[i].shape[0]
        slot = (z * group + place.e) if lines[i] else place.e
        cp = pltpu.make_async_copy(ins[i], outs[i].at[pl.ds(slot * rows, rows)], own.at[i])
        cp.start()
        copies_own.append(cp)
    greet(place, any(lines), owners)

    def block(i, rel, e, part=None):
        rows = ins[i].shape[0]
        slot = ((z + rel) * group + e) if lines[i] else e
        start, size = (0, rows) if part is None else part
        return outs[i].at[pl.ds(slot * rows + start, size)]

    def source(i, rel, part=None):
        if rel == 0:
            return ins[i] if part is None else ins[i].at[pl.ds(*part)]
        return block(i, rel, place.e, part)

    def sem(rel):
        return rel + owners - 1

    def go(i, rel, kind, src, dst, to_e, dz=0):
        return pltpu.make_async_remote_copy(
            src_ref=src, dst_ref=dst, send_sem=send.at[i, sem(rel), kind],
            recv_sem=recv.at[i, sem(rel - dz), min(kind, UP)],
            device_id=(z + dz, to_e), device_id_type=MESH)

    def parts(i):
        rows = ins[i].shape[0]
        return (0, halves[i]), (halves[i], rows - halves[i])

    def valid(rel):
        return (z + rel >= 0) & (z + rel < owners)

    def copies(i, rel):
        first, second = parts(i)
        e, xn, yn, dg, sb = place.e, place.xnb, place.ynb, place.diag, place.sib
        return {
            XS: lambda: go(i, rel, XS, source(i, rel), block(i, rel, e), xn),
            YS: lambda: go(i, rel, YS, source(i, rel), block(i, rel, e), yn),
            FA: lambda: go(i, rel, FA, block(i, rel, xn, first), block(i, rel, xn, first), yn),
            FB: lambda: go(i, rel, FB, block(i, rel, yn, second), block(i, rel, yn, second), xn),
            S0: lambda: go(i, rel, S0, source(i, rel), block(i, rel, e), sb),
            S1: lambda: go(i, rel, S1, block(i, rel, xn), block(i, rel, xn), sb),
            S2: lambda: go(i, rel, S2, block(i, rel, yn), block(i, rel, yn), sb),
            S3: lambda: go(i, rel, S3, block(i, rel, dg), block(i, rel, dg), sb),
        }

    def got(i, rel, kind, e, part=None):
        ref = block(i, rel, e, part)
        pltpu.make_async_remote_copy(
            src_ref=ref, dst_ref=ref, send_sem=send.at[i, sem(rel), min(kind, UP)], recv_sem=recv.at[i, sem(rel), min(kind, UP)],
            device_id=(z, place.sib), device_id_type=MESH).wait_recv()

    def stage_z(rel):
        @pl.when(valid(rel))
        def _():
            for i in range(n):
                if rel != 0 and not lines[i]:
                    continue
                if rel != 0:
                    got(i, rel, UP, place.e)
                if lines[i] and rel <= 0 and rel > 1 - owners:
                    @pl.when(z < owners - 1)
                    def _():
                        go(i, rel, UP, source(i, rel), block(i, rel, place.e), place.e, 1).start()
                if lines[i] and rel >= 0 and rel < owners - 1:
                    @pl.when(z > 0)
                    def _():
                        go(i, rel, DOWN, source(i, rel), block(i, rel, place.e), place.e, -1).start()
                c = copies(i, rel)
                c[XS]().start()
                c[YS]().start()
                c[S0]().start()

    def each(rel, fn):
        @pl.when(valid(rel))
        def _():
            for i in range(n):
                if rel == 0 or lines[i]:
                    fn(i, rel, copies(i, rel))

    def xy(i, rel, c):
        got(i, rel, XS, place.xnb)
        c[FA]().start()
        c[S1]().start()
        got(i, rel, YS, place.ynb)
        c[FB]().start()
        c[S2]().start()

    def dg(i, rel, c):
        first, second = parts(i)
        got(i, rel, FA, place.diag, first)
        got(i, rel, FB, place.diag, second)
        c[S3]().start()

    def end(i, rel, c):
        for k, e in ((S0, place.sib),):
            got(i, rel, S0, place.sib)
        got(i, rel, S1, place.xnb + place.sib - place.e)
        got(i, rel, S2, place.ynb + place.sib - place.e)
        got(i, rel, S3, place.diag + place.sib - place.e)
        for k in (XS, YS, FA, FB, S0, S1, S2, S3):
            c[k]().wait_send()
        if lines[i] and rel <= 0 and rel > 1 - owners:
            @pl.when(z < owners - 1)
            def _():
                go(i, rel, UP, source(i, rel), block(i, rel, place.e), place.e, 1).wait_send()
        if lines[i] and rel >= 0 and rel < owners - 1:
            @pl.when(z > 0)
            def _():
                go(i, rel, DOWN, source(i, rel), block(i, rel, place.e), place.e, -1).wait_send()

    rels = [0] + [s * d for d in range(1, owners) for s in (-1, 1)]
    waves = [[0]] + [[-d, d] for d in range(1, owners)]
    for w in range(owners + 3):
        if w < owners:
            for r in waves[w]:
                stage_z(r)
        if 0 <= w - 1 < owners:
            for r in waves[w - 1]:
                each(r, xy)
        if 0 <= w - 2 < owners:
            for r in waves[w - 2]:
                each(r, dg)
    for cp in copies_own:
        cp.wait()
    for r in rels:
        each(r, end)


def gather(arrays, lines, halves, owners, group, cid):
    outs = [jax.ShapeDtypeStruct((a.shape[0] * (owners if l else 1) * group,) + a.shape[1:], a.dtype) for a, l in zip(arrays, lines)]
    n = len(arrays)
    any_spec = pl.BlockSpec(memory_space=pl.ANY)
    return pl.pallas_call(
        functools.partial(gather_kernel, owners, group, lines, halves),
        out_shape=outs, in_specs=[any_spec] * n, out_specs=[any_spec] * n,
        scratch_shapes=[pltpu.SemaphoreType.DMA((n, 2 * owners - 1, 10)), pltpu.SemaphoreType.DMA((n, 2 * owners - 1, 9)), pltpu.SemaphoreType.DMA((n,))],
        compiler_params=pltpu.CompilerParams(collective_id=cid, has_side_effects=True),
    )(*arrays)


G = 16
(LOAD, SIB, Y0, Y1, X0, X1, X2, Y2, UP, DOWN) = range(10)


def scatter_kernel(owners, lines, subs, *refs):
    n = len(lines)
    ins, outs, scratch = refs[:n], refs[n : 2 * n], refs[2 * n :]
    send, recv = scratch[6 * n :]
    place = Place()
    z = place.z
    chips = {k: e // 2 for k, e in (("me", place.e), ("xn", place.xnb), ("yn", place.ynb), ("dg", place.diag))}

    class Item:
        def __init__(self, i, rel, sub):
            self.i, self.rel = i, rel
            self.line = lines[i]
            self.own, self.sib, self.first, self.second, self.up, self.down = scratch[6 * i : 6 * i + 6]
            groups, _, wide = ins[i].shape[3:]
            self.groups, self.half = groups, (groups + 1) // 2
            self.at = z + rel if self.line else 0
            width = wide // subs[i]
            self.cols = pl.ds(sub * width, width)
            self.slot = rel + owners - 1 if self.line else sub
            self.valid = (z + rel >= 0) & (z + rel < owners)

        def piece(self, ref, *lead):
            return ref.at[(*lead, slice(None), self.cols)]

        def rows(self, second):
            return pl.ds(self.half, self.groups - self.half) if second else pl.ds(0, self.half)

        def copy(self, kind, src, dst, to, dz=0):
            there = self.slot - dz if self.line else self.slot
            return pltpu.make_async_remote_copy(
                src_ref=src, dst_ref=dst,
                send_sem=send.at[self.i, self.slot, kind], recv_sem=recv.at[self.i, there, kind],
                device_id=(z + dz, to), device_id_type=MESH)

        def load(self):
            return pltpu.make_async_copy(
                self.piece(ins[self.i], self.at, slice(None), place.core, slice(None)),
                self.piece(self.own, self.at, slice(None), slice(None)),
                send.at[self.i, self.slot, LOAD])

        def to_sib(self):
            return self.copy(SIB, self.piece(ins[self.i], self.at, slice(None), 1 - place.core, slice(None)),
                             self.piece(self.sib, self.at, slice(None), slice(None)), place.sib)

        def hop1(self, axis, other):
            second = axis == 1
            to = place.xnb if axis else place.ynb
            whose = chips["dg"] if other else chips["xn" if axis else "yn"]
            size = self.groups - self.half if second else self.half
            return self.copy((X0, X1)[other] if axis else (Y0, Y1)[other],
                             self.piece(self.own, self.at, whose, self.rows(second)),
                             self.piece(self.first, self.at, axis, other, pl.ds(0, size)), to)

        def hop2(self, second):
            to = place.ynb if second else place.xnb
            whose = chips["yn" if second else "xn"]
            size = self.groups - self.half if second else self.half
            return self.copy(Y2 if second else X2,
                             self.piece(self.own, self.at, whose, self.rows(second)),
                             self.piece(self.second, self.at, int(second), pl.ds(0, size)), to)

        def along(self, up):
            return self.copy(UP if up else DOWN, self.piece(self.own, self.at, chips["me"], slice(None)),
                             self.piece(self.up if up else self.down, self.at, slice(None)), place.e, 1 if up else -1)

        def arrive_along(self, up):
            buf = self.piece(self.up if up else self.down, self.at, slice(None))
            pltpu.make_async_remote_copy(
                src_ref=buf, dst_ref=buf, send_sem=send.at[self.i, self.slot, UP if up else DOWN],
                recv_sem=recv.at[self.i, self.slot, UP if up else DOWN],
                device_id=(z, place.sib), device_id_type=MESH).wait_recv()

        def add(self, whose, start, count, terms, keep=None):
            own, cols, at = self.own, self.cols, self.at

            @pl.loop(0, count)
            def _(g):
                total = own[at, whose, start + g, :, cols].astype(F32)
                for ref, lead in terms:
                    total = total + ref[(*lead, g, slice(None), cols)].astype(F32)
                if keep is None:
                    own[at, whose, start + g, :, cols] = total.astype(BF)
                else:
                    keep[start + g, :, cols] = total

        def stage1(self):
            self.load().wait()
            self.to_sib().wait_recv()

            @pl.loop(0, 4)
            def _(chip):
                self.add(chip, 0, self.groups, [(self.sib, (self.at, chip))])
            for axis in (0, 1):
                for other in (1, 0):
                    self.hop1(axis, other).start()

        def stage2(self):
            self.hop1(0, 1).wait_recv()
            self.add(chips["xn"], 0, self.half, [(self.first, (self.at, 0, 1))])
            self.hop2(False).start()
            self.hop1(1, 1).wait_recv()
            self.add(chips["yn"], self.half, self.groups - self.half, [(self.first, (self.at, 1, 1))])
            self.hop2(True).start()

        def stage3(self):
            for axis in (0, 1):
                self.hop1(axis, 0).wait_recv()
                self.hop2(axis == 1).wait_recv()
            out = outs[self.i]
            rel = self.rel
            last = None if self.line and rel != 0 else out
            for half in (0, 1):
                start = self.half if half else 0
                size = self.groups - self.half if half else self.half
                self.add(chips["me"], start, size, [(self.first, (self.at, half, 0)), (self.second, (self.at, half))], last)
            if not self.line:
                return
            for up in (True, False):
                if (rel >= 0) if up else (rel <= 0):
                    @pl.when((z > 0) if up else (z < owners - 1))
                    def _():
                        self.arrive_along(up)
                        buf = self.up if up else self.down

                        @pl.loop(0, self.groups)
                        def _(g):
                            more = buf[self.at, g, :, self.cols].astype(F32)
                            if rel == 0:
                                out[g, :, self.cols] += more
                            else:
                                where = (self.at, chips["me"], g, slice(None), self.cols)
                                self.own[where] = (self.own[where].astype(F32) + more).astype(BF)
            if rel != 0:
                self.along(rel > 0).start()

        def end(self):
            self.to_sib().wait_send()
            for axis in (0, 1):
                for other in (0, 1):
                    self.hop1(axis, other).wait_send()
                self.hop2(axis == 1).wait_send()
            if self.line and self.rel != 0:
                self.along(self.rel > 0).wait_send()

    waves = []
    for d in range(owners - 1, 0, -1):
        waves.append([Item(i, rel, 0) for rel in (d, -d) for i in range(n) if lines[i]])
    waves.append([Item(i, 0, 0) for i in range(n) if lines[i]])
    waves = [w for w in waves if w]
    for i in range(n):
        if not lines[i]:
            waves += [[Item(i, 0, sub)] for sub in range(subs[i])]

    def run(wave, name):
        for item in wave:
            if item.line and item.rel != 0:
                pl.when(item.valid)(getattr(item, name))
            else:
                getattr(item, name)()

    def begin(item):
        item.load().start()

    for wave in waves:
        for item in wave:
            item.begin = functools.partial(begin, item)
            item.begin_sib = functools.partial(lambda it: it.to_sib().start(), item)
    for wave in waves:
        run(wave, "begin")
    greet(place, any(lines), owners)
    for wave in waves:
        run(wave, "begin_sib")
    for w in range(len(waves) + 2):
        for lag, name in enumerate(("stage1", "stage2", "stage3")):
            if 0 <= w - lag < len(waves):
                run(waves[w - lag], name)
    for wave in waves:
        run(wave, "end")


def scatter(arrays, lines, subs, owners, cid):
    n = len(arrays)
    scratch, outs = [], []
    for a, line in zip(arrays, lines):
        zs = a.shape[0]
        groups, _, wide = a.shape[3:]
        half = (groups + 1) // 2
        zl = zs if line else 1
        lg = groups if line else 1
        scratch += [
            pltpu.VMEM((zs, 4, groups, G, wide), BF),
            pltpu.VMEM((zs, 4, groups, G, wide), BF),
            pltpu.VMEM((zs, 2, 2, half, G, wide), BF),
            pltpu.VMEM((zs, 2, half, G, wide), BF),
            pltpu.VMEM((zl, lg, G, wide if line else 128), BF),
            pltpu.VMEM((zl, lg, G, wide if line else 128), BF),
        ]
        outs.append(jax.ShapeDtypeStruct((groups, G, wide), F32))
    slots = max([2 * owners - 1 if any(lines) else 1] + list(subs))
    scratch += [pltpu.SemaphoreType.DMA((n, slots, 10)), pltpu.SemaphoreType.DMA((n, slots, 10))]
    return pl.pallas_call(
        functools.partial(scatter_kernel, owners, lines, subs),
        out_shape=outs,
        in_specs=[pl.BlockSpec(memory_space=pl.ANY)] * n,
        out_specs=[pl.BlockSpec(memory_space=pltpu.VMEM)] * n,
        scratch_shapes=scratch,
        compiler_params=pltpu.CompilerParams(collective_id=cid, has_side_effects=True, vmem_limit_bytes=60 * 1024 * 1024),
    )(*arrays)


def moe_kernel(
    steps,
    slots,
    chunk,
    m_ref,
    g_ref,
    member_ref,
    router_ref,
    order_ref,
    mine_ref,
    weights_ref,
    moe_ref,
    drow_ref,
    grads_ref,
    grouter_ref,
    router_s,
    gate_s,
    hg_s,
    dpre_s,
    mt_s,
    gt_s,
    gup_s,
    gdn_s,
    gr_s,
):
    step = pl.program_id(0)
    owners, _, share, units = weights_ref.shape
    per = chunk // F

    @pl.when(step == 0)
    def _():
        gup_s[...] = jnp.zeros_like(gup_s)
        gdn_s[...] = jnp.zeros_like(gdn_s)
        gr_s[...] = jnp.zeros_like(gr_s)
        router_s[...] = dot_nn(router_ref[...], order_ref[...]).astype(BF)

    mt_s[...] = m_ref[...].T
    gt_s[...] = g_ref[...].T
    sig = jax.nn.sigmoid(dot_nn(m_ref[...], router_s[...]))
    mask = dot_nn(member_ref[...], mine_ref[...])
    gate_s[...] = sig * mask
    root = math.sqrt(2.0 / math.pi)
    cube = 0.044715
    lane = lax.broadcasted_iota(jnp.int32, (1, F), 1)
    d_gate = jnp.zeros(gate_s.shape, F32)
    for c in range(units // chunk):
        cols = pl.ds(c * chunk, chunk)
        pre_all = dot_nn(m_ref[:, :share], weights_ref[0, 0, :, cols])
        back_all = dot_nn(g_ref[:, :share], weights_ref[0, 1, :, cols])
        for o in range(1, owners):
            part = pl.ds(o * share, share)
            pre_all += dot_nn(m_ref[:, part], weights_ref[o, 0, :, cols])
            back_all += dot_nn(g_ref[:, part], weights_ref[o, 1, :, cols])
        for j in range(per):
            slot = c * per + j
            part = slice(j * F, (j + 1) * F)
            pre = pre_all[:, part]
            back = back_all[:, part]
            square = pre * pre
            th = jnp.tanh(root * pre * (1.0 + cube * square))
            half = 0.5 * (1.0 + th)
            slope = half + (0.5 * root) * pre * (1.0 - th * th) * (1.0 + (3.0 * cube) * square)
            hidden = (pre * half).astype(BF).astype(F32)
            gate = gate_s[:, slot : slot + 1]
            d_one = jnp.sum(hidden * back, axis=1, keepdims=True)
            d_gate = d_gate + d_one * (lane == slot).astype(F32)
            where = pl.ds(slot * F, F)
            hg_s[:, where] = (gate * hidden).astype(BF)
            dpre_s[:, where] = (slope * (gate * back)).astype(BF)
    dlog = (d_gate * mask * sig * (1.0 - sig)).astype(BF)
    gr_s[...] += dot_nn(mt_s[...], dot_nt(dlog, order_ref[...]).astype(BF))
    for o in range(owners):
        where = pl.ds(o * share, share)
        moe_ref[:, where] = dot_nt(hg_s[...], weights_ref[o, 1]).astype(BF)
        drow_ref[:, where] = (
            dot_nt(dpre_s[...], weights_ref[o, 0]) + dot_nt(dlog, router_s[where, :])
        ).astype(BF)
        gup_s[where, :] += dot_nn(mt_s[where, :], dpre_s[...])
        gdn_s[where, :] += dot_nn(gt_s[where, :], hg_s[...])

    @pl.when(step == steps - 1)
    def _():
        for o in range(owners):
            grads_ref[o, 0] = gup_s[pl.ds(o * share, share), :].astype(BF)
            grads_ref[o, 1] = gdn_s[pl.ds(o * share, share), :].astype(BF)
        grouter_ref[...] = gr_s[...].astype(BF)


def moe(rows, cots, member, packed, router_at, order, mine, weights):
    count = rows.shape[0]
    tile = 512
    owners, _, share, units = weights.shape
    slots = units // F
    steps = count // tile
    lanes = member.shape[1]
    row_spec = pl.BlockSpec((tile, D), lambda i: (i, 0))
    whole = pl.BlockSpec(memory_space=pltpu.VMEM)
    router_spec = pl.BlockSpec((D, lanes), lambda i: (0, router_at // lanes))
    return pl.pallas_call(
        functools.partial(moe_kernel, steps, slots, 512),
        grid=(steps,),
        in_specs=[
            row_spec,
            row_spec,
            pl.BlockSpec((tile, lanes), lambda i: (i, 0)),
            router_spec,
            whole,
            whole,
            whole,
        ],
        out_specs=[row_spec, row_spec, whole, whole],
        out_shape=[
            jax.ShapeDtypeStruct((count, D), BF),
            jax.ShapeDtypeStruct((count, D), BF),
            jax.ShapeDtypeStruct(weights.shape, BF),
            jax.ShapeDtypeStruct((D, lanes), BF),
        ],
        scratch_shapes=[
            pltpu.VMEM((D, F), BF),
            pltpu.VMEM((tile, F), F32),
            pltpu.VMEM((tile, units), BF),
            pltpu.VMEM((tile, units), BF),
            pltpu.VMEM((D, tile), BF),
            pltpu.VMEM((D, tile), BF),
            pltpu.VMEM((D, units), F32),
            pltpu.VMEM((D, units), F32),
            pltpu.VMEM((D, lanes), F32),
        ],
        compiler_params=pltpu.CompilerParams(vmem_limit_bytes=60 * 1024 * 1024),
        cost_estimate=pl.CostEstimate(
            flops=12 * count * D * units,
            bytes_accessed=count * D * 8 + D * units * 8,
            transcendentals=count * units,
        ),
    )(rows, cots, member, packed, order, mine, weights)


def picked_mask(picks, number):
    return jnp.sum(
        (picks[..., None] == jnp.arange(number, dtype=jnp.int32)).astype(F32), axis=-2
    )


def layer_normed(inputs, gain_row):
    centred = inputs - jnp.mean(inputs, axis=-1, keepdims=True)
    variance = jnp.mean(centred * centred, axis=-1, keepdims=True)
    return centred * lax.rsqrt(variance + epsilon) * gain_row


def head_gates(select, value_mask, out_mask):
    row_count = value_mask.shape[0]
    value_gate = jax.nn.sigmoid(select[:, : H * NV]).reshape(row_count, H, NV) * value_mask
    out_gate = jax.nn.sigmoid(select[:, H * NV :]).reshape(row_count, H, NV) * out_mask
    return (value_gate, out_gate)


def dense_forward(tokens, live, lengths, picks, gain, qkv, select_w, heads):
    count = tokens.shape[0]
    seq = count // MB
    xf = tokens.astype(F32)
    value_mask = picked_mask(picks, NV)
    out_mask = value_mask * live[:, None, None]
    normed, norm_back = jax.vjp(layer_normed, xf, gain.astype(F32))
    normed_low = normed.astype(BF)
    query_key = dot_nn(normed_low, qkv[:, :QK]).astype(BF)
    values_all = dot_nn(tokens, qkv[:, QK:])
    select = dot_nn(tokens, select_w)
    (value_gate, out_gate), gate_back = jax.vjp(
        lambda logits_in: head_gates(logits_in, value_mask, out_mask), select
    )
    values_split = values_all.reshape(count, H, NV, HD)
    values_low = jnp.sum(value_gate[..., None] * values_split, axis=2).astype(BF)
    values_seq = values_low.reshape(MB, seq, H, HD)
    queries = query_key[:, : H * HD].reshape(MB, seq, H, HD)
    keys_all = query_key[:, H * HD :].reshape(MB, seq, H, HD)
    position = jnp.arange(seq, dtype=jnp.int32)
    scores = jnp.einsum("bihd,bjhd->bhij", queries, keys_all, preferred_element_type=F32) * HD ** (
        -0.5
    )
    allowed = (position[None, :] <= position[:, None])[None] & (
        position[None, None, :] < lengths[:, None, None]
    )
    masked = jnp.where(allowed[:, None], scores, -1e30)
    expo = jnp.exp(masked - jnp.max(masked, axis=-1, keepdims=True))
    attention = expo / jnp.sum(expo, axis=-1, keepdims=True)
    attended = jnp.einsum(
        "bhij,bjhd->bihd", attention.astype(BF), values_seq, preferred_element_type=F32
    ).reshape(count, H, HD)
    mixed_heads = (out_gate[..., None] * attended[:, :, None, :]).reshape(count, VAL).astype(BF)
    middle = xf + dot_nn(mixed_heads, heads)

    def backward(d_middle):
        d_branch = d_middle.astype(BF)
        grad_heads = dot_tn(mixed_heads, d_branch)
        d_mixed = dot_nt(d_branch, heads).reshape(count, H, NV, HD)
        d_attended = jnp.sum(out_gate[..., None] * d_mixed, axis=2).astype(BF)
        d_out_gate = jnp.sum(d_mixed * attended[:, :, None, :], axis=-1)
        d_att_seq = d_attended.reshape(MB, seq, H, HD)
        d_attention = jnp.einsum(
            "bihd,bjhd->bhij", d_att_seq, values_seq, preferred_element_type=F32
        )
        d_scores = (
            attention * (d_attention - jnp.sum(attention * d_attention, axis=-1, keepdims=True))
        ).astype(BF)
        d_values = (
            jnp.einsum(
                "bhij,bihd->bjhd", attention.astype(BF), d_att_seq, preferred_element_type=F32
            )
            .astype(BF)
            .reshape(count, H, HD)
        )
        d_queries = jnp.einsum(
            "bhij,bjhd->bihd", d_scores, keys_all, preferred_element_type=F32
        ) * HD ** (-0.5)
        d_keys = jnp.einsum(
            "bhij,bihd->bjhd", d_scores, queries, preferred_element_type=F32
        ) * HD ** (-0.5)
        d_query_key = jnp.concatenate(
            [d_queries.reshape(count, H * HD), d_keys.reshape(count, H * HD)], axis=1
        ).astype(BF)
        d_value_gate = jnp.sum(d_values[:, :, None, :] * values_split, axis=-1)
        d_values_all = (value_gate[..., None] * d_values[:, :, None, :]).reshape(count, VAL).astype(BF)
        d_select = gate_back((d_value_gate, d_out_gate))[0].astype(BF)
        grad_qk = dot_tn(normed_low, d_query_key)
        grad_val = dot_tn(tokens, d_values_all)
        grad_select = dot_tn(tokens, d_select)
        d_normed = dot_nt(d_query_key, qkv[:, :QK])
        d_norm_in, grad_gain = norm_back(d_normed)
        d_tokens = (
            d_middle
            + d_norm_in
            + dot_nt(d_values_all, qkv[:, QK:])
            + dot_nt(d_select, select_w)
        )
        return d_tokens, grad_gain, grad_qk, grad_val, grad_select, grad_heads

    return middle, backward


def body(
    tokens,
    cotangent,
    lengths,
    routes,
    head_choice,
    placement,
    gain_master,
    gain_moment,
    gain_average,
    qkv_master,
    qkv_moment,
    qkv_average,
    select_master,
    select_moment,
    select_average,
    router_master,
    router_moment,
    router_average,
    heads_out_master,
    heads_out_moment,
    heads_out_average,
    up_master,
    up_moment,
    up_average,
    down_master,
    down_moment,
    down_average,
):
    both = ("dp", "expert")
    owners = lax.axis_size("dp")
    group = lax.axis_size("expert")
    own_kernels = group == 8
    experts = placement.shape[0]
    slots = up_master.shape[0]
    units = slots * F
    seq = tokens.shape[1]
    count = MB * seq
    share = up_master.shape[1]
    mine = lax.axis_index("expert")
    lanes = -(-experts // 128) * 128

    own_rows = qkv_master.shape[0]
    wide = QK + VAL
    packed = jnp.concatenate(
        [
            qkv_master.astype(BF),
            router_master.astype(BF),
            jnp.zeros((own_rows, lanes - experts), BF),
            select_master.astype(BF),
            gain_master.astype(BF)[:, None],
            jnp.zeros((own_rows, 127 - SEL), BF),
        ],
        axis=1,
    )
    heads_low = heads_out_master.astype(BF)

    def flat(weights):
        return weights.astype(BF).transpose(1, 0, 2).reshape(share, units)

    experts_low = jnp.concatenate([flat(up_master), flat(down_master)], axis=0)
    experts_all = lax.all_gather(experts_low, "dp", axis=0, tiled=False)
    weights = experts_all.reshape(owners, 2, share, units)

    flat_tokens = tokens.reshape(count, D)
    flat_cots = cotangent.reshape(count, D)
    live = (jnp.arange(seq, dtype=jnp.int32)[None, :] < lengths).astype(F32).reshape(count)
    lane_ids = jnp.arange(lanes, dtype=jnp.int32)
    named = jnp.sum(
        (routes.reshape(count, TOPK)[..., None] == lane_ids).astype(F32), axis=1
    ) * live[:, None]
    padded = jnp.pad(placement, (0, lanes - experts), constant_values=-1)
    perm = (padded[:, None] == lane_ids[None, :]).astype(BF)
    member = dot_nn(named.astype(BF), perm).astype(BF)
    own_lane = jnp.arange(F, dtype=jnp.int32)[None, :]
    mine_sel = (((lane_ids[:, None] - mine * slots) == own_lane) & (own_lane < slots)).astype(BF)
    order_mine = (
        ((padded[:, None] - mine * slots) == own_lane) & (own_lane < slots) & (padded[:, None] >= 0)
    ).astype(BF)

    if own_kernels:
        packed_all, heads, cots_all, member_all = gather(
            (packed, heads_low, flat_cots, member),
            (True, True, False, False),
            (own_rows // 2, 48, count // 2, count // 2),
            owners,
            group,
            0,
        )
    else:
        packed_all = lax.all_gather(packed, both, axis=0, tiled=True)
        heads = lax.all_gather(heads_low, both, axis=0, tiled=True)
        cots_all = lax.all_gather(flat_cots, "expert", axis=0, tiled=True)
        member_all = lax.all_gather(member, "expert", axis=0, tiled=True)
    qkv = packed_all[:, :wide]
    select_w = packed_all[:, wide + lanes : wide + lanes + SEL]
    gain = packed_all[:, wide + lanes + SEL]

    middle, backward = dense_forward(
        flat_tokens,
        live,
        lengths[:, 0],
        head_choice.reshape(count, H, -1),
        gain,
        qkv,
        select_w,
        heads,
    )
    middle_low = middle.astype(BF)
    if own_kernels:
        (rows_all,) = gather((middle_low,), (False,), (count // 2,), owners, group, 1)
    else:
        rows_all = lax.all_gather(middle_low, "expert", axis=0, tiled=True)
    moe_part, drow_part, expert_grads, grad_router = moe(
        rows_all, cots_all, member_all, packed_all, wide, order_mine, mine_sel, weights
    )
    expert_sum = lax.psum_scatter(
        expert_grads.reshape(owners * 2 * share, units), "dp", scatter_dimension=0, tiled=True
    ).astype(F32)
    if own_kernels:
        (d_from_rows,) = scatter((drow_part.reshape(1, 4, 2, count // G, G, D),), (False,), (4,), owners, 2)
        d_from_rows = d_from_rows.reshape(count, D)
    else:
        d_from_rows = lax.psum_scatter(drow_part, "expert", scatter_dimension=0, tiled=True).astype(F32)
    moe_sum = lax.psum_scatter(moe_part, "expert", scatter_dimension=0, tiled=True).astype(F32)
    mixed = (middle + moe_sum).astype(BF)

    d_middle = flat_cots.astype(F32) + d_from_rows
    d_tokens, grad_gain, grad_qk, grad_val, grad_select, grad_heads = backward(d_middle)
    small_grads = jnp.concatenate(
        [
            grad_router,
            grad_select.astype(BF),
            grad_gain.astype(BF)[:, None],
            jnp.zeros((D, 127 - SEL), BF),
        ],
        axis=1,
    )
    dense_grads = (grad_qk.astype(BF), grad_val.astype(BF), small_grads, grad_heads.astype(BF))
    if own_kernels:
        sums = scatter(
            tuple(g.reshape(owners, 4, 2, -1, G, g.shape[1]) for g in dense_grads),
            (True,) * 4,
            (1,) * 4,
            owners,
            3,
        )
        qk_sum, val_sum, small_sum, heads_sum = (s.reshape(-1, s.shape[2]) for s in sums)
    else:
        qk_sum, val_sum, small_sum, heads_sum = (
            lax.psum_scatter(g, both, scatter_dimension=0, tiled=True).astype(F32)
            for g in dense_grads
        )
    qkv_sum = jnp.concatenate([qk_sum, val_sum], axis=1)
    router_sum = small_sum[:, :experts]
    select_sum = small_sum[:, lanes : lanes + SEL]
    gain_sum = small_sum[:, lanes + SEL]
    up_sum = expert_sum[:share].reshape(share, slots, F).transpose(1, 0, 2)
    down_sum = expert_sum[share:].reshape(share, slots, F).transpose(1, 0, 2)

    rates = step_rates(count * owners * group, experts)
    outs = (
        update_weight(gain_master, gain_moment, gain_average, gain_sum, rates[0])
        + update_weight(qkv_master, qkv_moment, qkv_average, qkv_sum, rates[1])
        + update_weight(select_master, select_moment, select_average, select_sum, rates[2])
        + update_weight(router_master, router_moment, router_average, router_sum, rates[3])
        + update_weight(heads_out_master, heads_out_moment, heads_out_average, heads_sum, rates[4])
        + update_weight(up_master, up_moment, up_average, up_sum, rates[5])
        + update_weight(down_master, down_moment, down_average, down_sum, rates[6])
    )
    return (mixed.reshape(tokens.shape), d_tokens.reshape(tokens.shape)) + outs


def solution(mesh):
    rows = P(None, ("dp", "expert"), None)
    flat = P(("dp", "expert"))
    dense = P(("dp", "expert"), None)
    expert = P("expert", "dp", None)
    in_specs = (
        rows,
        rows,
        P(None, ("dp", "expert")),
        rows,
        P(None, ("dp", "expert"), None, None),
        P(),
        *((flat,) * 3),
        *((dense,) * 12),
        *((expert,) * 6),
    )
    out_specs = (rows, rows, *((flat,) * 4), *((dense,) * 16), *((expert,) * 8))
    return jax.shard_map(body, mesh=mesh, in_specs=in_specs, out_specs=out_specs, check_vma=False)
```

time: 1940 us -> 558 us (0.29)
  waiting for transfers between devices: 951 us -> 0.05 us
  local copies, waits for them, and re-layouts: 493 us -> 84.8 us
  Pallas kernels: 0 us -> 351 us
  blocking collectives: 161 us -> 0 us
  matrix products: 159 us -> 58.8 us
  other arithmetic: 103 us -> 42.8 us
  starting transfers between devices: 41.8 us -> 0.12 us
    reduce_scatter x7 -> x2, waiting for transfers between devices: 488 us -> 0.01 us  [the longest x1 0.01 us: body(): lax.psum_scatter(moe_part, 'expert', scatter_dimension=0, tiled=True)]
    all_to_all x8 -> x0, waiting for transfers between devices: 400 us -> none  [the longest x2 155 us: micro_step(): lax.all_to_all(d_rows.reshape(axis_count, exp_dev * most, D), 'expert', s...]
    pallas_call x0 -> x5, Pallas kernels: none -> 351 us  [the longest x2 135 us: gather(): pl.pallas_call(functools.partial(gather_kernel, owners, group, lines, hal...]
    gather x40 -> x0, local copies, waits for them, and re-layouts: 257 us -> none  [the longest x2 40.9 us: micro_step(): rows_back.reshape(experts * most, D)[destination]]
    scatter x6 -> x0, local copies, waits for them, and re-layouts: 155 us -> none  [the longest x2 91.8 us: micro_step(): jnp.zeros((experts * most, D), jnp.bfloat16).at[destination]]
    dot_general x56 -> x18, matrix products: 159 us -> 56.6 us  [the longest x4 19.2 us: dot_nt(): lax.dot_general(a, b, (((1,), (1,)), ((), ())), preferred_element_type=F32)]
    unnamed x2 -> x0, blocking collectives: 82.2 us -> none
    all_gather x2 -> x0, blocking collectives: 78.7 us -> none  [the longest x1 40.9 us: fetch_dense(): lax.all_gather(select_low, ('dp', 'expert'), axis=0, tiled=True)]
  transfers between devices with their start and end apart: 20 -> 3, of which waited for: 12 -> 0; matrix products, arithmetic and copies ran while one was open for 35% -> 23% of each run, Pallas kernels for 0% -> 48%
where the time goes in v1:
time: 558 us; the launch traced here: 553 us
  Pallas kernels  351 us (63%)
  local copies, waits for them, and re-layouts  84.8 us (15%)
  matrix products  58.8 us (11%)
  other arithmetic  42.8 us (8%)
  between operations  14.9 us (3%)
    pallas_call x2, Pallas kernels, gather(): pl.pallas_call(functools.partial(gather_kernel, owners, group, lines, hal...  135 us
    pallas_call x2, Pallas kernels, scatter(): pl.pallas_call(functools.partial(scatter_kernel, owners, lines, subs), ou...  129 us
    pallas_call x1, Pallas kernels, moe(): pl.pallas_call(functools.partial(moe_kernel, steps, slots, 512), grid=(st...  86.8 us
    unnamed x171, local copies, waits for them, and re-layouts  45.4 us
    dot_general x4, matrix products, dot_nt(): lax.dot_general(a, b, (((1,), (1,)), ((), ())), preferred_element_type=F32)  19.2 us
    dot_general x5, matrix products, dot_nn(): return jnp.dot(a, b, preferred_element_type=F32)  16.1 us
    dot_general x4, matrix products, dot_tn(): lax.dot_general(a, b, (((0,), (0,)), ((), ())), preferred_element_type=F32)  14.6 us
  transfers between devices with their start and end apart: 3, of which 0 were waited for; matrix products, arithmetic and copies ran while one was open for 23% of the time, Pallas kernels for 48%

profile of v1, /device:TPU:0, one launch (start us, length us, event | category | flops | bytes accessed | tf_op | source)
XLA Modules:
  0.0 552.5 jit_solution(13439303677043731228)
XLA Ops:
  9.2 3.5 copy.165
  22.1 101.6 %shard_map.490 = (bf16[1024,3840]{1,0:T(8,128)(2,1)}, bf16[2560,1024]{1,0:T(8,128)(2,1)}, bf16[3072,1024]{1,0:T(8,128)(2,1)}, bf16[3072,128]{1,0:T(8,128)(2,1)}) custom-call(bf16[32,3840]{1,0:T(8,128)(2,1)} %concatenate.21.refs_0_, bf16[80,1024]{1,0:T(8,128)(2,1)} %convert_element_type.234.refs_1_, bf16[384,1024]{1,0:T(8,128)(2,1)} %bitcast.132, ...), custom_call_target="tpu_custom_call" | custom-call | tf_op jit(solution)/shard_map/pallas_call | solution.py:249
  126.5 4.9 fusion.3
  136.2 2.9 fusion.25
  146.5 6.1 %fusion.93 = (bf16[384,1024]{1,0:T(8,128)(2,1)}, f32[384,1024]{1,0:T(8,128)}) fusion(bf16[384,2560]{0,1:T(8,128)(2,1)S(1)} %bitcast.130, bf16[2560,1024]{1,0:T(8,128)(2,1)} %get-tuple-element.43, bf16[384,1024]{1,0:T(8,128)(2,1)S(1)} %bitcast.124), kind=kOutput, calls=%fused_computation.161 | convolution fusion | flops 2014445568 | bytes 10354688 | tf_op jit(solution)/shard_map/dot_general | solution.py:65
  152.7 33.8 %shard_map.491.m_ref = bf16[3072,1024]{1,0:T(8,128)(2,1)} custom-call(bf16[384,1024]{1,0:T(8,128)(2,1)} %get-tuple-element.191.refs_0_), custom_call_target="tpu_custom_call" | custom-call | tf_op jit(solution)/shard_map/pallas_call | solution.py:249
  187.2 8.7 %copy.167 = bf16[2048,1536]{1,0:T(8,128)(2,1)} copy(bf16[2048,1536]{0,1:T(8,128)(2,1)} %all-gather.3.cloned.1.call-done) | data formatting | bytes 12582912 | tf_op jit(solution)/shard_map/all_gather | solution.py:771
  195.9 86.8 %shard_map.492 = (bf16[3072,1024]{1,0:T(8,128)(2,1)}, bf16[3072,1024]{1,0:T(8,128)(2,1)}, bf16[4,2,256,1536]{3,2,1,0:T(8,128)(2,1)}, bf16[1024,128]{1,0:T(8,128)(2,1)}) custom-call(bf16[3072,1024]{1,0:T(8,128)(2,1)} %shard_map.491.m_ref, bf16[3072,1024]{1,0:T(8,128)(2,1)} %get-tuple-element.44.g_ref, bf16[3072,128]{1,0:T(8,128)(2,1)} %get-tuple-element.45.member_ref, ...), custom_call_target="tpu_custom_call" | custom-call | flops 57982058496 | bytes 37748736 | tf_op jit(solution)/shard_map/pallas_call | solution.py:569
  282.7 8.8 %copy.183 = bf16[2048,1536]{0,1:T(8,128)(2,1)} copy(bf16[2048,1536]{1,0:T(8,128)(2,1)} %bitcast.135) | data formatting | bytes 12582912 | tf_op jit(solution)/shard_map/reshape | solution.py:827
  292.9 3.2 copy.182
  296.2 3.1 copy.185
  299.3 3.0 copy.186
  302.3 3.1 copy.188
  306.0 44.7 %shard_map.493 = f32[24,16,1024]{2,1,0:T(8,128)} custom-call(bf16[1,4,2,24,16,1024]{5,4,3,2,1,0:T(8,128)(2,1)} %bitcast.137), custom_call_target="tpu_custom_call" | custom-call | tf_op jit(solution)/shard_map/pallas_call | solution.py:461
  352.4 6.6 %multiply_reduce_fusion.1 = (f32[384,4,5]{0,2,1:T(8,128)}, bf16[384,4,128]{0,2,1:T(8,128)(2,1)}) fusion(f32[384,4,128]{0,2,1:T(8,128)S(1)} %copy-done.12, f32[384,4,5]{0,2,1:T(8,128)S(1)} %copy-done.48, bf16[384,1024,1,1]{1,0,3,2:T(8,128)(2,1)S(1)} %bitcast.155, bf16[4,5,128,1024]{3,2,1,0:T(8,128)(2,1)} %bitcast.129), kind=kOutput, calls=%fused_computation.8 | convolution fusion | flops 2016993792 | bytes 7270400 | tf_op jit(solution)/shard_map/dot_general | solution.py:57
  366.1 2.9 multiply_reduce_fusion.4
  374.5 4.9 multiply_reduce_fusion
  382.9 4.8 fusion.16
  395.8 4.1 convolution_convert_fusion.2
  400.0 4.8 convolution_convert_fusion.1
  404.8 4.8 convolution_convert_fusion
  409.6 84.2 %shard_map.494 = (f32[2,16,1024]{2,1,0:T(8,128)}, f32[2,16,2560]{2,1,0:T(8,128)}, f32[2,16,256]{2,1,0:T(8,128)}, f32[5,16,1024]{2,1,0:T(8,128)}) custom-call(bf16[4,4,2,2,16,1024]{5,4,3,2,1,0:T(8,128)(2,1)} %bitcast.146, bf16[4,4,2,2,16,2560]{5,4,3,2,1,0:T(8,128)(2,1)} %bitcast.140, bf16[4,4,2,2,16,256]{5,4,3,2,1,0:T(8,128)(2,1)} %maximum_maximum_fusion.refs_2_, ...), custom_call_target="tpu_custom_call" | custom-call | tf_op jit(solution)/shard_map/pallas_call | solution.py:461
  500.8 4.9 fusion.1
  505.8 2.8 fusion.23
  512.8 2.9 fusion.86
  517.8 3.1 copy.189
  522.6 2.8 add_multiply_fusion.1
  525.4 3.0 copy.190
  530.1 4.0 fusion.77
  534.1 3.1 copy.193
  538.8 2.8 add_multiply_fusion
  541.6 3.0 copy.194
  (260 shorter events, 73.9 us)
Async XLA Ops:
  7.2 180.0 %all-gather.3.cloned.1.call-start = ((), (), s32[]{:S(2)}) async-start(), calls=%async_computation.4 | async-start | bytes 7864320 | tf_op jit(solution)/shard_map/all_gather | solution.py:771
  9.1 3.6 copy-start.3
  15.6 494.9 %reduce-scatter.3.cloned.1.call-start = ((), (), s32[]{:S(2)}) async-start(), calls=%async_computation.2 | async-start | bytes 7077888 | tf_op jit(solution)/shard_map/reduce_scatter | solution.py:834
  16.7 107.0 %copy-start = (bf16[2,192,1024]{2,1,0:T(8,128)(2,1)S(1)}, bf16[2,192,1024]{2,1,0:T(8,128)(2,1)}, u32[]{:S(2)}) copy-start(bf16[2,192,1024]{2,1,0:T(8,128)(2,1)} %param.27) | copy-start | bytes 2359300
  19.0 106.7 %copy-start.63 = (s32[2,192,4,2]{1,3,2,0:T(2,128)S(1)}, s32[2,192,4,2]{1,3,2,0:T(2,128)}, u32[]{:S(2)}) copy-start(s32[2,192,4,2]{1,3,2,0:T(2,128)} %param.31) | copy-start | bytes 36868
  126.5 5.0 copy-start.32
  133.9 8.5 %copy-start.33 = (bf16[384,4,128]{2,0,1:T(8,128)(2,1)}, bf16[384,4,128]{2,0,1:T(8,128)(2,1)S(1)}, u32[]{:S(2)}) copy-start(bf16[384,4,128]{2,0,1:T(8,128)(2,1)S(1)} %copy.158) | copy-start | bytes 1179652
  134.7 4.4 copy-start.59
  145.1 7.6 %copy-start.11 = (f32[384,4,128]{0,2,1:T(8,128)}, f32[384,4,128]{0,2,1:T(8,128)S(1)}, u32[]{:S(2)}) copy-start(f32[384,4,128]{0,2,1:T(8,128)S(1)} %copy.164) | copy-start | bytes 2359300
  152.6 33.8 %copy-start.72 = (s32[96]{0:T(128)S(1)}, s32[96]{0:T(128)}, u32[]{:S(2)}) copy-start(s32[96]{0:T(128)} %param.32) | copy-start | bytes 1156
  152.6 33.8 %copy-start.67 = (s32[128]{0:T(128)S(1)}, s32[128]{0:T(128)}, u32[]{:S(2)}) copy-start(s32[128]{0:T(128)} %get-tuple-element.185) | copy-start | bytes 1540
  152.6 33.8 %copy-start.68 = (s32[128]{0:T(128)S(1)}, s32[128]{0:T(128)}, u32[]{:S(2)}) copy-start(s32[128]{0:T(128)} %get-tuple-element.196) | copy-start | bytes 1540
  282.7 230.1 %reduce-scatter.5.cloned.1.call-start = ((), (), s32[]{:S(2)}) async-start(), calls=%async_computation.3 | async-start | bytes 7864320 | tf_op jit(solution)/shard_map/reduce_scatter | solution.py:826
  306.0 44.7 %copy-start.8 = (bf16[2,192,1024]{2,1,0:T(8,128)(2,1)S(1)}, bf16[2,192,1024]{2,1,0:T(8,128)(2,1)}, u32[]{:S(2)}) copy-start(bf16[2,192,1024]{2,1,0:T(8,128)(2,1)} %param.28) | copy-start | bytes 2359300
  352.4 6.7 %copy-start.27 = (bf16[24,16,1024]{2,1,0:T(8,128)(2,1)}, bf16[24,16,1024]{2,1,0:T(8,128)(2,1)S(1)}, u32[]{:S(2)}) copy-start(bf16[24,16,1024]{2,1,0:T(8,128)(2,1)S(1)} %fusion.20) | copy-start | bytes 2359300
  382.9 4.8 copy-start.46
  395.8 4.1 copy-start.13
  400.0 4.8 copy-start.28
  409.6 85.2 %copy-start.74 = (f32[32]{0:T(128)S(1)}, f32[32]{0:T(128)}, u32[]{:S(2)}) copy-start(f32[32]{0:T(128)} %param.33) | copy-start | bytes 388
  409.6 85.2 %copy-start.75 = (f32[32]{0:T(128)S(1)}, f32[32]{0:T(128)}, u32[]{:S(2)}) copy-start(f32[32]{0:T(128)} %param.34) | copy-start | bytes 388
  409.6 85.7 %copy-start.77 = (f32[32]{0:T(128)S(1)}, f32[32]{0:T(128)}, u32[]{:S(2)}) copy-start(f32[32]{0:T(128)} %param.35) | copy-start | bytes 388
  409.6 86.2 %copy-start.60 = (f32[384]{0:T(512)S(1)}, f32[384]{0:T(512)}, u32[]{:S(2)}) copy-start(f32[384]{0:T(512)} %copy-done.59) | copy-start | bytes 4612
  409.6 86.2 %copy-start.69 = (f32[384]{0:T(512)S(1)}, f32[384]{0:T(512)}, u32[]{:S(2)}) copy-start(f32[384]{0:T(512)} %get-tuple-element.147) | copy-start | bytes 4612
  409.6 86.2 %copy-start.18 = (f32[384,1024]{1,0:T(8,128)S(1)}, f32[384,1024]{1,0:T(8,128)}, u32[]{:S(2)}) copy-start(f32[384,1024]{1,0:T(8,128)} %get-tuple-element.195) | copy-start | bytes 4718596
  495.9 3.1 copy-start.24
  495.9 4.0 copy-start.43
  496.5 4.3 copy-start.14
  497.2 8.5 %copy-start.52 = (f32[32,40]{1,0:T(8,128)}, f32[32,40]{1,0:T(8,128)S(1)}, u32[]{:S(2)}) copy-start(f32[32,40]{1,0:T(8,128)S(1)} %get-tuple-element.159) | copy-start | bytes 15364
  500.0 5.8 %copy-start.25 = (f32[80,1024]{1,0:T(8,128)}, f32[80,1024]{1,0:T(8,128)S(1)}, u32[]{:S(2)}) copy-start(f32[80,1024]{1,0:T(8,128)S(1)} %get-tuple-element.153) | copy-start | bytes 983044
  500.8 4.9 copy-start.2
  500.8 5.0 copy-start.37
  500.8 5.0 copy-start.39
  (49 other events, 90.1 us)
Sparse Core Ops, SparseCore 0:
  15.7 139.4 all-gather.2
  282.8 75.4 reduce-scatter.2
  360.7 135.3 reduce-scatter.4

commit v2 on v1

--- a/solution.py
+++ b/solution.py
@@ -605,6 +605,350 @@
     )(rows, cots, member, packed, order, mine, weights)
 
 
+def fused_kernel(owners, slots, wide, tile_cols, *refs):
+    middle, cots, member, weights, packed, order_ref, mine_ref = refs[:7]
+    drow_out, moe_out, grads_out, grouter_out = refs[7:11]
+    (m_s, c_s, b_s, w_s, gup_s, gdn_s, gr_s, hg_s, dpre_s, mt_s, gt_s, router_in, router_s, gate_s) = refs[11:25]
+    (sib_s, first_s, second_s, gsend, grecv, ssend, srecv, local, wsem) = refs[25:]
+    place = Place()
+    z = place.z
+    count = middle.shape[0]
+    half = count // 2
+    lanes = b_s.shape[1]
+    share = D // owners
+    ins = (member, middle, cots)
+    bufs = (b_s, m_s, c_s)
+    sums = (m_s, c_s)
+    swap = place.sib - place.e
+    mine = (place.e, place.xnb, place.ynb, place.diag)
+
+    def span(e, start=0, size=count):
+        return pl.ds(pl.multiple_of(e * count + start, 16), size)
+
+    def remote(sems, a, kind, src, dst, to):
+        return pltpu.make_async_remote_copy(
+            src_ref=src, dst_ref=dst, send_sem=sems[0].at[a, kind], recv_sem=sems[1].at[a, kind],
+            device_id=(z, to), device_id_type=MESH)
+
+    def passing(a, kind):
+        buf = bufs[a]
+        if kind in (XS, YS, S0):
+            src, at = ins[a], span(place.e)
+        elif kind == FA:
+            at = span(place.xnb, 0, half)
+            src = buf.at[at]
+        elif kind == FB:
+            at = span(place.ynb, half, half)
+            src = buf.at[at]
+        else:
+            at = span(mine[kind - S0])
+            src = buf.at[at]
+        to = {XS: place.xnb, YS: place.ynb, FA: place.ynb, FB: place.xnb}.get(kind, place.sib)
+        return remote((gsend, grecv), a, kind, src, buf.at[at], to)
+
+    def got(a, kind):
+        at = {
+            XS: lambda: span(place.xnb),
+            YS: lambda: span(place.ynb),
+            FA: lambda: span(place.diag, 0, half),
+            FB: lambda: span(place.diag, half, half),
+        }.get(kind, lambda: span(mine[kind - S0] + swap))()
+        ref = bufs[a].at[at]
+        remote((gsend, grecv), a, kind, ref, ref, place.sib).wait_recv()
+
+    HY0, HY1, HX0, HX1, HX2, HY2 = 4, 5, 6, 7, 8, 9
+
+    def to_sib(a, t):
+        return remote((ssend, srecv), a, t, sums[a].at[span(mine[t] + swap)], sib_s.at[a, t], place.sib)
+
+    def hop(a, kind):
+        src_e, second, dst, to = {
+            HY0: (place.ynb, False, first_s.at[a, 0], place.ynb),
+            HY1: (place.diag, False, first_s.at[a, 1], place.ynb),
+            HX0: (place.xnb, True, first_s.at[a, 2], place.xnb),
+            HX1: (place.diag, True, first_s.at[a, 3], place.xnb),
+            HX2: (place.xnb, False, second_s.at[a, 0], place.xnb),
+            HY2: (place.ynb, True, second_s.at[a, 1], place.ynb),
+        }[kind]
+        src = sums[a].at[span(src_e, half if second else 0, half)]
+        return remote((ssend, srecv), a, kind, src, dst, to)
+
+    step_rows = 32
+
+    def add(a, e, start, size, terms, keep=None):
+        buf = sums[a]
+
+        @pl.loop(0, size // step_rows)
+        def _(g):
+            here = pl.ds(pl.multiple_of(e * count + start + g * step_rows, 16), step_rows)
+            there = pl.ds(pl.multiple_of(g * step_rows, 16), step_rows)
+            total = buf[here, :].astype(F32)
+            for lead in terms:
+                total = total + lead[0][(*lead[1], there, slice(None))].astype(F32)
+            if keep is None:
+                buf[here, :] = total.astype(BF)
+            else:
+                keep[pl.ds(pl.multiple_of(start + g * step_rows, 16), step_rows), :] = total
+
+    def with_sib(t):
+        for a in (0, 1):
+            to_sib(a, t).wait_recv()
+            add(a, mine[t], 0, count, [(sib_s, (a, t))])
+
+    own = [
+        pltpu.make_async_copy(ins[a], bufs[a].at[span(place.e)], local.at[a]) for a in range(3)
+    ]
+    for c in own:
+        c.start()
+    router_copy = pltpu.make_async_copy(packed.at[:, pl.ds(wide, lanes)], router_in, local.at[3])
+    router_copy.start()
+
+    @pl.loop(0, slots)
+    def _(s):
+        for o in range(owners):
+            for k in (0, 1):
+                pltpu.make_async_copy(
+                    weights.at[o, k * slots + s],
+                    w_s.at[k, pl.ds(o * share, share), pl.ds(pl.multiple_of(s * F, F), F)],
+                    wsem.at[0],
+                ).start()
+
+    greet(place, False, owners)
+    for a in range(3):
+        for kind in (XS, YS, S0):
+            passing(a, kind).start()
+    gup_s[...] = jnp.zeros_like(gup_s)
+    gdn_s[...] = jnp.zeros_like(gdn_s)
+    gr_s[...] = jnp.zeros_like(gr_s)
+
+    root = math.sqrt(2.0 / math.pi)
+    cube = 0.044715
+    tile = 2 * count
+    units = slots * F
+    per = tile_cols // F
+
+    @pl.loop(0, 4)
+    def _(t):
+        @pl.when(t == 0)
+        def _():
+            for c in own:
+                c.wait()
+            router_copy.wait()
+            router_s[...] = dot_nn(router_in[...], order_ref[...]).astype(BF)
+            for a in range(3):
+                got(a, S0)
+            pltpu.make_async_copy(w_s, w_s, wsem.at[0]).wait()
+
+        @pl.when(t == 1)
+        def _():
+            for a in range(3):
+                got(a, XS)
+                passing(a, FA).start()
+                passing(a, S1).start()
+                got(a, YS)
+                passing(a, FB).start()
+                passing(a, S2).start()
+            for a in range(3):
+                got(a, S1)
+
+        @pl.when(t == 2)
+        def _():
+            for a in range(3):
+                got(a, FA)
+                got(a, FB)
+                passing(a, S3).start()
+            for a in range(3):
+                got(a, S2)
+
+        @pl.when(t == 3)
+        def _():
+            for a in range(3):
+                got(a, S3)
+
+        tx, ty = t % 2, t // 2
+        chip_x = place.x + tx * (1 - 2 * place.x)
+        chip_y = place.y + ty * (1 - 2 * place.y)
+        chip = chip_y * 2 + chip_x
+        here = pl.ds(pl.multiple_of(chip * tile, 16), tile)
+        mt_s[...] = m_s[here, :].T
+        gt_s[...] = c_s[here, :].T
+        sig = jax.nn.sigmoid(dot_nn(m_s[here, :], router_s[...]))
+        mask = dot_nn(b_s[here, :], mine_ref[...])
+        gate_s[...] = sig * mask
+        lane = lax.broadcasted_iota(jnp.int32, (1, F), 1)
+        d_gate = jnp.zeros(gate_s.shape, F32)
+        for c in range(units // tile_cols):
+            cols = pl.ds(c * tile_cols, tile_cols)
+            pre_all = dot_nn(m_s[here, :], w_s[0, :, cols])
+            back_all = dot_nn(c_s[here, :], w_s[1, :, cols])
+            for j in range(per):
+                slot = c * per + j
+                part = slice(j * F, (j + 1) * F)
+                pre = pre_all[:, part]
+                back = back_all[:, part]
+                square = pre * pre
+                th = jnp.tanh(root * pre * (1.0 + cube * square))
+                halved = 0.5 * (1.0 + th)
+                slope = halved + (0.5 * root) * pre * (1.0 - th * th) * (1.0 + (3.0 * cube) * square)
+                hidden = (pre * halved).astype(BF).astype(F32)
+                gate = gate_s[:, slot : slot + 1]
+                d_one = jnp.sum(hidden * back, axis=1, keepdims=True)
+                d_gate = d_gate + d_one * (lane == slot).astype(F32)
+                where = pl.ds(slot * F, F)
+                hg_s[:, where] = (gate * hidden).astype(BF)
+                dpre_s[:, where] = (slope * (gate * back)).astype(BF)
+        dlog = (d_gate * mask * sig * (1.0 - sig)).astype(BF)
+        gr_s[...] += dot_nn(mt_s[...], dot_nt(dlog, order_ref[...]).astype(BF))
+
+        @pl.when(t == 1)
+        def _():
+            with_sib(0)
+            for a in range(3):
+                passing(a, FA).wait_send()
+                passing(a, S1).wait_send()
+
+        @pl.when(t == 2)
+        def _():
+            with_sib(1)
+            for a in (0, 1):
+                hop(a, HX0).start()
+            for a in range(3):
+                passing(a, FB).wait_send()
+                passing(a, S2).wait_send()
+
+        @pl.when(t == 3)
+        def _():
+            with_sib(2)
+            for a in (0, 1):
+                hop(a, HY0).start()
+            for a in range(3):
+                passing(a, S3).wait_send()
+
+        for n in range(D // 256):
+            where = pl.ds(n * 256, 256)
+            m_s[here, where] = (
+                dot_nt(dpre_s[...], w_s[0, where, :]) + dot_nt(dlog, router_s[where, :])
+            ).astype(BF)
+        for k in range(4):
+
+            @pl.when(t == k)
+            def _():
+                to_sib(0, k).start()
+
+        for n in range(D // 256):
+            where = pl.ds(n * 256, 256)
+            c_s[here, where] = dot_nt(hg_s[...], w_s[1, where, :]).astype(BF)
+        for k in range(4):
+
+            @pl.when(t == k)
+            def _():
+                to_sib(1, k).start()
+
+        for n in range(D // 256):
+            where = pl.ds(n * 256, 256)
+            gup_s[where, :] += dot_nn(mt_s[where, :], dpre_s[...])
+            gdn_s[where, :] += dot_nn(gt_s[where, :], hg_s[...])
+
+    for a in (0, 1):
+        to_sib(a, 3).wait_recv()
+        add(a, mine[3], 0, count, [(sib_s, (a, 3))])
+        hop(a, HY1).start()
+        hop(a, HX1).start()
+    w_s[0] = gup_s[...].astype(BF)
+    w_s[1] = gdn_s[...].astype(BF)
+
+    @pl.loop(0, slots)
+    def _(s):
+        for o in range(owners):
+            for k in (0, 1):
+                pltpu.make_async_copy(
+                    w_s.at[k, pl.ds(o * share, share), pl.ds(pl.multiple_of(s * F, F), F)],
+                    grads_out.at[o, k * slots + s],
+                    wsem.at[0],
+                ).start()
+
+    grouter_out[...] = gr_s[...].astype(BF)
+    for a in (0, 1):
+        hop(a, HY1).wait_recv()
+        add(a, place.xnb, 0, half, [(first_s, (a, 1))])
+        hop(a, HX2).start()
+        hop(a, HX1).wait_recv()
+        add(a, place.ynb, half, half, [(first_s, (a, 3))])
+        hop(a, HY2).start()
+    for a, out in ((0, drow_out), (1, moe_out)):
+        hop(a, HY0).wait_recv()
+        hop(a, HX2).wait_recv()
+        add(a, place.e, 0, half, [(first_s, (a, 0)), (second_s, (a, 0))], out)
+        hop(a, HX0).wait_recv()
+        hop(a, HY2).wait_recv()
+        add(a, place.e, half, half, [(first_s, (a, 2)), (second_s, (a, 1))], out)
+    for a in range(3):
+        for kind in (XS, YS, S0):
+            passing(a, kind).wait_send()
+    for a in (0, 1):
+        for t in range(4):
+            to_sib(a, t).wait_send()
+        for kind in (HY0, HY1, HX0, HX1, HX2, HY2):
+            hop(a, kind).wait_send()
+    pltpu.make_async_copy(w_s, w_s, wsem.at[0]).wait()
+
+
+def fused_experts(middle, cots, member, weights, packed, wide, order, mine, cid):
+    count = middle.shape[0]
+    owners = weights.shape[0]
+    slots = weights.shape[1] // 2
+    lanes = member.shape[1]
+    units = slots * F
+    tile = 2 * count
+    hbm = pl.BlockSpec(memory_space=pl.ANY)
+    vmem = pl.BlockSpec(memory_space=pltpu.VMEM)
+    dma = pltpu.SemaphoreType.DMA
+    return pl.pallas_call(
+        functools.partial(fused_kernel, owners, slots, wide, 256),
+        in_specs=[hbm] * 5 + [vmem] * 2,
+        out_specs=[vmem, vmem, hbm, vmem],
+        out_shape=[
+            jax.ShapeDtypeStruct((count, D), F32),
+            jax.ShapeDtypeStruct((count, D), F32),
+            jax.ShapeDtypeStruct(weights.shape, BF),
+            jax.ShapeDtypeStruct((D, lanes), BF),
+        ],
+        scratch_shapes=[
+            pltpu.VMEM((8 * count, D), BF),
+            pltpu.VMEM((8 * count, D), BF),
+            pltpu.VMEM((8 * count, lanes), BF),
+            pltpu.VMEM((2, D, units), BF),
+            pltpu.VMEM((D, units), F32),
+            pltpu.VMEM((D, units), F32),
+            pltpu.VMEM((D, lanes), F32),
+            pltpu.VMEM((tile, units), BF),
+            pltpu.VMEM((tile, units), BF),
+            pltpu.VMEM((D, tile), BF),
+            pltpu.VMEM((D, tile), BF),
+            pltpu.VMEM((D, lanes), BF),
+            pltpu.VMEM((D, F), BF),
+            pltpu.VMEM((tile, F), F32),
+            pltpu.VMEM((2, 4, count, D), BF),
+            pltpu.VMEM((2, 4, count // 2, D), BF),
+            pltpu.VMEM((2, 2, count // 2, D), BF),
+            dma((3, 8)),
+            dma((3, 8)),
+            dma((2, 10)),
+            dma((2, 10)),
+            dma((4,)),
+            dma((1,)),
+        ],
+        compiler_params=pltpu.CompilerParams(
+            collective_id=cid, has_side_effects=True, vmem_limit_bytes=64 * 1024 * 1024 - 65536
+        ),
+        cost_estimate=pl.CostEstimate(
+            flops=12 * 8 * count * D * units,
+            bytes_accessed=D * units * 8,
+            transcendentals=8 * count * units,
+        ),
+    )(middle, cots, member, weights, packed, order, mine)
+
+
 def picked_mask(picks, number):
     return jnp.sum(
         (picks[..., None] == jnp.arange(number, dtype=jnp.int32)).astype(F32), axis=-2
@@ -764,12 +1108,8 @@
     )
     heads_low = heads_out_master.astype(BF)
 
-    def flat(weights):
-        return weights.astype(BF).transpose(1, 0, 2).reshape(share, units)
-
-    experts_low = jnp.concatenate([flat(up_master), flat(down_master)], axis=0)
-    experts_all = lax.all_gather(experts_low, "dp", axis=0, tiled=False)
-    weights = experts_all.reshape(owners, 2, share, units)
+    experts_low = jnp.concatenate([up_master.astype(BF), down_master.astype(BF)], axis=0)
+    weights = lax.all_gather(experts_low, "dp", axis=0, tiled=False)
 
     flat_tokens = tokens.reshape(count, D)
     flat_cots = cotangent.reshape(count, D)
@@ -788,19 +1128,12 @@
     ).astype(BF)
 
     if own_kernels:
-        packed_all, heads, cots_all, member_all = gather(
-            (packed, heads_low, flat_cots, member),
-            (True, True, False, False),
-            (own_rows // 2, 48, count // 2, count // 2),
-            owners,
-            group,
-            0,
+        packed_all, heads = gather(
+            (packed, heads_low), (True, True), (own_rows // 2, 48), owners, group, 0
         )
     else:
         packed_all = lax.all_gather(packed, both, axis=0, tiled=True)
         heads = lax.all_gather(heads_low, both, axis=0, tiled=True)
-        cots_all = lax.all_gather(flat_cots, "expert", axis=0, tiled=True)
-        member_all = lax.all_gather(member, "expert", axis=0, tiled=True)
     qkv = packed_all[:, :wide]
     select_w = packed_all[:, wide + lanes : wide + lanes + SEL]
     gain = packed_all[:, wide + lanes + SEL]
@@ -817,21 +1150,32 @@
     )
     middle_low = middle.astype(BF)
     if own_kernels:
-        (rows_all,) = gather((middle_low,), (False,), (count // 2,), owners, group, 1)
+        d_from_rows, moe_sum, expert_grads, grad_router = fused_experts(
+            middle_low, flat_cots, member, weights, packed_all, wide, order_mine, mine_sel, 1
+        )
     else:
-        rows_all = lax.all_gather(middle_low, "expert", axis=0, tiled=True)
-    moe_part, drow_part, expert_grads, grad_router = moe(
-        rows_all, cots_all, member_all, packed_all, wide, order_mine, mine_sel, weights
-    )
+        rows_all, cots_all, member_all = (
+            lax.all_gather(a, "expert", axis=0, tiled=True) for a in (middle_low, flat_cots, member)
+        )
+        side = weights.reshape(owners, 2, slots, share, F).transpose(0, 1, 3, 2, 4)
+        moe_part, drow_part, expert_grads, grad_router = moe(
+            rows_all,
+            cots_all,
+            member_all,
+            packed_all,
+            wide,
+            order_mine,
+            mine_sel,
+            side.reshape(owners, 2, share, units),
+        )
+        expert_grads = expert_grads.reshape(owners, 2, share, slots, F).transpose(0, 1, 3, 2, 4)
+        d_from_rows, moe_sum = (
+            lax.psum_scatter(a, "expert", scatter_dimension=0, tiled=True).astype(F32)
+            for a in (drow_part, moe_part)
+        )
     expert_sum = lax.psum_scatter(
-        expert_grads.reshape(owners * 2 * share, units), "dp", scatter_dimension=0, tiled=True
+        expert_grads.reshape(owners * 2 * slots, share, F), "dp", scatter_dimension=0, tiled=True
     ).astype(F32)
-    if own_kernels:
-        (d_from_rows,) = scatter((drow_part.reshape(1, 4, 2, count // G, G, D),), (False,), (4,), owners, 2)
-        d_from_rows = d_from_rows.reshape(count, D)
-    else:
-        d_from_rows = lax.psum_scatter(drow_part, "expert", scatter_dimension=0, tiled=True).astype(F32)
-    moe_sum = lax.psum_scatter(moe_part, "expert", scatter_dimension=0, tiled=True).astype(F32)
     mixed = (middle + moe_sum).astype(BF)
 
     d_middle = flat_cots.astype(F32) + d_from_rows
@@ -864,8 +1208,8 @@
     router_sum = small_sum[:, :experts]
     select_sum = small_sum[:, lanes : lanes + SEL]
     gain_sum = small_sum[:, lanes + SEL]
-    up_sum = expert_sum[:share].reshape(share, slots, F).transpose(1, 0, 2)
-    down_sum = expert_sum[share:].reshape(share, slots, F).transpose(1, 0, 2)
+    up_sum = expert_sum[:slots]
+    down_sum = expert_sum[slots:]
 
     rates = step_rates(count * owners * group, experts)
     outs = (

time: 558 us -> 483 us (0.87)
  local copies, waits for them, and re-layouts: 84.8 us -> 25.1 us
  Pallas kernels: 351 us -> 324 us
  other arithmetic: 42.8 us -> 54.8 us
    pallas_call x1, Pallas kernels: 86.8 us -> 150 us  [fused_experts(): pl.pallas_call(functools.partial(fused_kernel, owners, slots, wide, 256),...]
    pallas_call x2 -> x1, Pallas kernels: 129 us -> 82.9 us  [scatter(): pl.pallas_call(functools.partial(scatter_kernel, owners, lines, subs), ou...]
    pallas_call x2 -> x1, Pallas kernels: 135 us -> 90.7 us  [gather(): pl.pallas_call(functools.partial(gather_kernel, owners, group, lines, hal...]
    unnamed x171 -> x177, local copies, waits for them, and re-layouts: 45.4 us -> 10.7 us
    reduce_sum x1, other arithmetic: 2.19 us -> 15.5 us  [body(): jnp.sum((routes.reshape(count, TOPK)[..., None] == lane_ids).astype(F32),...]
    reshape x1 -> x0, local copies, waits for them, and re-layouts: 8.81 us -> none  [body(): expert_grads.reshape(owners * 2 * share, units)]
    all_gather x1 -> x0, local copies, waits for them, and re-layouts: 8.66 us -> none  [body(): experts_all = lax.all_gather(experts_low, 'dp', axis=0, tiled=False)]
  transfers between devices with their start and end apart: 3 -> 2, of which waited for: 0 -> 0; matrix products, arithmetic and copies ran while one was open for 23% -> 24% of each run, Pallas kernels for 48% -> 36%
where the time goes in v2:
time: 483 us; the launch traced here: 478 us
  Pallas kernels  324 us (67%)
  matrix products  58.5 us (12%)
  other arithmetic  54.8 us (11%)
  local copies, waits for them, and re-layouts  25.1 us (5%)
  between operations  15.4 us (3%)
    pallas_call x1, Pallas kernels, fused_experts(): pl.pallas_call(functools.partial(fused_kernel, owners, slots, wide, 256),...  150 us
    pallas_call x1, Pallas kernels, gather(): pl.pallas_call(functools.partial(gather_kernel, owners, group, lines, hal...  90.7 us
    pallas_call x1, Pallas kernels, scatter(): pl.pallas_call(functools.partial(scatter_kernel, owners, lines, subs), ou...  82.9 us
    dot_general x5, matrix products, dot_nn(): return jnp.dot(a, b, preferred_element_type=F32)  18.7 us
    dot_general x4, matrix products, dot_nt(): lax.dot_general(a, b, (((1,), (1,)), ((), ())), preferred_element_type=F32)  18.4 us
    reduce_sum x1, other arithmetic, body(): jnp.sum((routes.reshape(count, TOPK)[..., None] == lane_ids).astype(F32),...  15.5 us
    dot_general x4, matrix products, dot_tn(): lax.dot_general(a, b, (((0,), (0,)), ((), ())), preferred_element_type=F32)  14.6 us
    unnamed x177, local copies, waits for them, and re-layouts  10.7 us
  transfers between devices with their start and end apart: 2, of which 0 were waited for; matrix products, arithmetic and copies ran while one was open for 24% of the time, Pallas kernels for 36%

profile of v2, /device:TPU:0, one launch (start us, length us, event | category | flops | bytes accessed | tf_op | source)
XLA Modules:
  0.0 477.7 jit_solution(8147768861048162807)
XLA Ops:
  7.3 1.6 convert_element_type.232
  9.2 1.3 pad_maximum_fusion
  13.2 90.7 %shard_map.490 = (bf16[1024,3840]{1,0:T(8,128)(2,1)}, bf16[2560,1024]{1,0:T(8,128)(2,1)}) custom-call(bf16[32,3840]{1,0:T(8,128)(2,1)} %concatenate.21.refs_0_, bf16[80,1024]{1,0:T(8,128)(2,1)} %convert_element_type.213.refs_1_), custom_call_target="tpu_custom_call" | custom-call | tf_op jit(solution)/shard_map/pallas_call | solution.py:249
  104.0 1.3 convolution_bitcast_fusion.1
  106.9 7.5 %fusion.3 = f32[2560,384]{1,0:T(8,128)} fusion(bf16[384,1024]{1,0:T(8,128)(2,1)S(1)} %bitcast.96, bf16[1024,3840]{1,0:T(8,128)(2,1)} %get-tuple-element.40.refs_4_), kind=kOutput, calls=%fused_computation.5 | convolution fusion | flops 2013265920 | bytes 9961472 | tf_op jit(solution)/shard_map/dot_general | solution.py:65
  114.4 2.5 multiply_reduce_fusion.3
  120.0 2.9 fusion.21
  124.0 1.6 fusion.84
  128.2 15.5 %convert_reduce_fusion = f32[384,128]{1,0:T(8,128)S(1)} fusion(s32[384,16]{1,0:T(8,128)S(1)} %bitcast.117), kind=kLoop, calls=%fused_computation.13 | loop fusion | flops 2310144 | bytes 221184 | tf_op jit(solution)/shard_map/reduce_sum | solution.py:1118
  147.0 6.1 %fusion.89 = (bf16[384,1024]{1,0:T(8,128)(2,1)}, f32[384,1024]{1,0:T(8,128)}) fusion(bf16[384,2560]{0,1:T(8,128)(2,1)S(1)} %bitcast.100, bf16[2560,1024]{1,0:T(8,128)(2,1)} %get-tuple-element.41, bf16[384,1024]{1,0:T(8,128)(2,1)S(1)} %bitcast.97), kind=kOutput, calls=%fused_computation.157 | convolution fusion | flops 2014445568 | bytes 10354688 | tf_op jit(solution)/shard_map/dot_general | solution.py:65
  153.2 150.2 %shard_map.491 = (f32[384,1024]{1,0:T(8,128)}, f32[384,1024]{1,0:T(8,128)}, bf16[4,24,256,128]{3,2,1,0:T(8,128)(2,1)}, bf16[1024,128]{1,0:T(8,128)(2,1)}) custom-call(bf16[384,1024]{1,0:T(8,128)(2,1)} %get-tuple-element.98.refs_0_, bf16[384,1024]{1,0:T(8,128)(2,1)} %bitcast.106, bf16[384,128]{1,0:T(8,128)(2,1)} %convolution_convert_fusion.4.refs_2_, ...), custom_call_target="tpu_custom_call" | custom-call | flops 57982058496 | bytes 12582912 | tf_op jit(solution)/shard_map/pallas_call | solution.py:906
  305.7 5.9 %fusion.90 = f32[384,2560]{0,1:T(8,128)S(1)} fusion(bf16[384,1024]{1,0:T(8,128)(2,1)S(1)} %fusion.31, bf16[2560,1024]{1,0:T(8,128)(2,1)} %get-tuple-element.41), kind=kOutput, calls=%fused_computation.158 | convolution fusion | flops 2013265920 | bytes 9961472 | tf_op jit(solution)/shard_map/dot_general | solution.py:57
  313.1 1.9 fusion.27
  316.0 1.4 copy.143
  317.4 2.0 multiply_reduce_fusion.4
  322.9 1.4 reduce_sum.146
  324.3 4.6 multiply_reduce_fusion
  328.9 1.5 reduce_sum.149
  331.6 4.8 %fusion.16 = (bf16[1024]{0:T(1024)(128)(2,1)S(1)}, f32[384]{0:T(512)}, f32[384,1024]{1,0:T(8,128)}) fusion(f32[384]{0:T(512)S(1)} %copy-done.69, f32[384]{0:T(512)S(1)} %copy-done.67, bf16[2,192,1024]{2,1,0:T(8,128)(2,1)S(1)} %copy-done.1, f32[1024]{0:T(1024)S(1)} %copy-done.62, bf16[384,1024]{1,0:T(8,128)(2,1)S(1)} %bitcast_dynamic-update-slice_fusion, ...), kind=kOutput, calls=%fused_computation.32 | convolution fusion | flops 808450688 | bytes 5253632 | tf_op jit(solution)/shard_map/dot_general | solution.py:57
  338.6 1.7 copy.145
  340.4 2.0 maximum_maximum_fusion.refs_2_
  342.4 4.2 convolution_convert_fusion.2
  346.6 4.6 convolution_convert_fusion
  351.2 4.9 %convolution_convert_fusion.1 = bf16[2560,1024]{0,1:T(8,128)(2,1)} fusion(bf16[384,2560]{0,1:T(8,128)(2,1)S(1)} %bitcast.111, bf16[384,1024]{1,0:T(8,128)(2,1)S(1)} %bitcast.99), kind=kOutput, calls=%fused_computation.2 | convolution fusion | flops 2015887360 | bytes 7995392 | tf_op jit(solution)/shard_map/dot_general | solution.py:61
  356.2 82.9 %shard_map.492 = (f32[2,16,1024]{2,1,0:T(8,128)}, f32[2,16,2560]{2,1,0:T(8,128)}, f32[2,16,256]{2,1,0:T(8,128)}, f32[5,16,1024]{2,1,0:T(8,128)}) custom-call(bf16[4,4,2,2,16,1024]{5,4,3,2,1,0:T(8,128)(2,1)} %bitcast.110, bf16[4,4,2,2,16,2560]{5,4,3,2,1,0:T(8,128)(2,1)} %bitcast.104, bf16[4,4,2,2,16,256]{5,4,3,2,1,0:T(8,128)(2,1)} %maximum_maximum_fusion.refs_2_, ...), custom_call_target="tpu_custom_call" | custom-call | tf_op jit(solution)/shard_map/pallas_call | solution.py:461
  441.2 2.2 fusion.82
  449.5 4.8 %fusion.1 = f32[384,1024]{1,0:T(8,128)S(1)} fusion(bf16[384,2560]{0,1:T(8,128)(2,1)S(1)} %bitcast.112, bf16[1024,3840]{1,0:T(8,128)(2,1)} %get-tuple-element.40.refs_4_), kind=kOutput, calls=%fused_computation.3 | convolution fusion | flops 2013265920 | bytes 8781824 | tf_op jit(solution)/shard_map/dot_general | solution.py:57
  454.3 2.8 add_add_fusion.1
  459.7 1.9 convert_element_type.261
  462.5 4.3 fusion.74
  466.8 1.3 add_multiply_fusion.1
  469.4 1.3 add_multiply_fusion
  (259 shorter events, 38.6 us)
Async XLA Ops:
  7.2 145.9 %all-gather.3.cloned.1.call-start = ((), (), s32[]{:S(2)}) async-start(), calls=%async_computation.2 | async-start | bytes 7864320 | tf_op jit(solution)/shard_map/all_gather | solution.py:1112
  10.5 93.4 %copy-start = (bf16[2,192,1024]{2,1,0:T(8,128)(2,1)S(1)}, bf16[2,192,1024]{2,1,0:T(8,128)(2,1)}, u32[]{:S(2)}) copy-start(bf16[2,192,1024]{2,1,0:T(8,128)(2,1)} %param.27) | copy-start | bytes 2359300
  10.6 449.2 %reduce-scatter.2.cloned.1.call-start = ((), (), s32[]{:S(2)}) async-start(), calls=%async_computation.1 | async-start | bytes 7864320 | tf_op jit(solution)/shard_map/reduce_scatter | solution.py:1176
  11.5 94.4 %copy-start.75 = (s32[2,192,4,2]{1,3,2,0:T(2,128)S(1)}, s32[2,192,4,2]{1,3,2,0:T(2,128)}, u32[]{:S(2)}) copy-start(s32[2,192,4,2]{1,3,2,0:T(2,128)} %param.31) | copy-start | bytes 36868
  11.6 94.5 %copy-start.81 = (s32[2,1]{0,1:T(1,128)S(1)}, s32[2,1]{0,1:T(1,128)}, u32[]{:S(2)}) copy-start(s32[2,1]{0,1:T(1,128)} %param.29) | copy-start | bytes 28
  106.2 38.2 %copy-start.63 = (f32[384]{0:T(512)}, f32[384]{0:T(512)S(1)}, u32[]{:S(2)}) copy-start(f32[384]{0:T(512)S(1)} %reshape.356) | copy-start | bytes 4612
  106.9 7.5 %copy-start.37 = (f32[384,4,5]{0,2,1:T(8,128)}, f32[384,4,5]{0,2,1:T(8,128)S(1)}, u32[]{:S(2)}) copy-start(f32[384,4,5]{0,2,1:T(8,128)S(1)} %copy.122) | copy-start | bytes 92164
  117.1 8.5 %copy-start.40 = (bf16[384,4,128]{2,0,1:T(8,128)(2,1)}, bf16[384,4,128]{2,0,1:T(8,128)(2,1)S(1)}, u32[]{:S(2)}) copy-start(bf16[384,4,128]{2,0,1:T(8,128)(2,1)S(1)} %copy.123) | copy-start | bytes 1179652
  117.4 5.5 %copy-start.66 = (f32[384]{0:T(512)}, f32[384]{0:T(512)S(1)}, u32[]{:S(2)}) copy-start(f32[384]{0:T(512)S(1)} %div.37) | copy-start | bytes 4612
  117.8 5.0 %copy-start.71 = (f32[384]{0:T(512)}, f32[384]{0:T(512)S(1)}, u32[]{:S(2)}) copy-start(f32[384]{0:T(512)S(1)} %add.122) | copy-start | bytes 4612
  117.8 5.0 %copy-start.68 = (f32[384]{0:T(512)}, f32[384]{0:T(512)S(1)}, u32[]{:S(2)}) copy-start(f32[384]{0:T(512)S(1)} %rsqrt.10) | copy-start | bytes 4612
  127.6 18.1 %copy-start.4 = (f32[384,4,128]{0,2,1:T(8,128)}, f32[384,4,128]{0,2,1:T(8,128)S(1)}, u32[]{:S(2)}) copy-start(f32[384,4,128]{0,2,1:T(8,128)S(1)} %copy.129) | copy-start | bytes 2359300
  128.0 17.7 %copy-start.38 = (f32[384,4,5]{0,2,1:T(8,128)}, f32[384,4,5]{0,2,1:T(8,128)S(1)}, u32[]{:S(2)}) copy-start(f32[384,4,5]{0,2,1:T(8,128)S(1)} %copy.120) | copy-start | bytes 92164
  305.6 6.0 %copy-start.31 = (bf16[384,1024]{1,0:T(8,128)(2,1)}, bf16[384,1024]{1,0:T(8,128)(2,1)S(1)}, u32[]{:S(2)}) copy-start(bf16[384,1024]{1,0:T(8,128)(2,1)S(1)} %fusion.31) | copy-start | bytes 2359300
  305.7 6.0 %copy-start.5 = (f32[384,4,128]{0,2,1:T(8,128)S(1)}, f32[384,4,128]{0,2,1:T(8,128)}, u32[]{:S(2)}) copy-start(f32[384,4,128]{0,2,1:T(8,128)} %copy-done.4) | copy-start | bytes 2359300
  305.7 6.0 %copy-start.39 = (f32[384,4,5]{0,2,1:T(8,128)S(1)}, f32[384,4,5]{0,2,1:T(8,128)}, u32[]{:S(2)}) copy-start(f32[384,4,5]{0,2,1:T(8,128)} %copy-done.38) | copy-start | bytes 92164
  331.5 4.9 %copy-start.51 = (bf16[384,1024]{1,0:T(8,128)(2,1)}, bf16[384,1024]{1,0:T(8,128)(2,1)S(1)}, u32[]{:S(2)}) copy-start(bf16[384,1024]{1,0:T(8,128)(2,1)S(1)} %bitcast_dynamic-update-slice_fusion) | copy-start | bytes 2359300
  331.6 5.3 %copy-start.34 = (f32[384,40]{0,1:T(8,128)S(1)}, f32[384,40]{0,1:T(8,128)}, u32[]{:S(2)}) copy-start(f32[384,40]{0,1:T(8,128)} %copy-done.33) | copy-start | bytes 184324
  331.6 5.3 %copy-start.64 = (f32[384]{0:T(512)S(1)}, f32[384]{0:T(512)}, u32[]{:S(2)}) copy-start(f32[384]{0:T(512)} %copy-done.63) | copy-start | bytes 4612
  346.6 4.6 copy-start.14
  356.1 83.8 %copy-start.84 = (f32[32]{0:T(128)S(1)}, f32[32]{0:T(128)}, u32[]{:S(2)}) copy-start(f32[32]{0:T(128)} %param.33) | copy-start | bytes 388
  356.2 83.8 %copy-start.85 = (f32[32]{0:T(128)S(1)}, f32[32]{0:T(128)}, u32[]{:S(2)}) copy-start(f32[32]{0:T(128)} %param.34) | copy-start | bytes 388
  356.2 84.4 %copy-start.87 = (f32[32]{0:T(128)S(1)}, f32[32]{0:T(128)}, u32[]{:S(2)}) copy-start(f32[32]{0:T(128)} %param.35) | copy-start | bytes 388
  356.2 84.9 %copy-start.72 = (f32[384]{0:T(512)S(1)}, f32[384]{0:T(512)}, u32[]{:S(2)}) copy-start(f32[384]{0:T(512)} %copy-done.71) | copy-start | bytes 4612
  356.2 84.9 %copy-start.80 = (f32[384]{0:T(512)S(1)}, f32[384]{0:T(512)}, u32[]{:S(2)}) copy-start(f32[384]{0:T(512)} %get-tuple-element.53) | copy-start | bytes 4612
  356.2 84.9 %copy-start.70 = (f32[384]{0:T(512)S(1)}, f32[384]{0:T(512)}, u32[]{:S(2)}) copy-start(f32[384]{0:T(512)} %copy-done.68) | copy-start | bytes 4612
  441.2 4.8 copy-start.28
  441.2 4.8 copy-start.45
  441.2 4.7 copy-start.47
  441.2 6.5 %copy-start.24 = (f32[384,1024]{1,0:T(8,128)S(1)}, f32[384,1024]{1,0:T(8,128)}, u32[]{:S(2)}) copy-start(f32[384,1024]{1,0:T(8,128)} %get-tuple-element.42) | copy-start | bytes 4718596
  443.4 4.3 copy-start.9
  462.5 4.3 copy-start.22
  (58 other events, 115.8 us)
Sparse Core Ops, SparseCore 0:
  10.7 135.5 all-gather.2
  303.5 132.6 reduce-scatter.1

commit v3 on v2

--- a/solution.py
+++ b/solution.py
@@ -616,8 +616,8 @@
     half = count // 2
     lanes = b_s.shape[1]
     share = D // owners
-    ins = (member, middle, cots)
-    bufs = (b_s, m_s, c_s)
+    ins = (middle,)
+    bufs = (m_s,)
     sums = (m_s, c_s)
     swap = place.sib - place.e
     mine = (place.e, place.xnb, place.ynb, place.diag)
@@ -696,7 +696,11 @@
             add(a, mine[t], 0, count, [(sib_s, (a, t))])
 
     own = [
-        pltpu.make_async_copy(ins[a], bufs[a].at[span(place.e)], local.at[a]) for a in range(3)
+        pltpu.make_async_copy(ins[a], bufs[a].at[span(place.e)], local.at[a]) for a in range(1)
+    ]
+    own += [
+        pltpu.make_async_copy(cots, c_s, local.at[1]),
+        pltpu.make_async_copy(member, b_s, local.at[2]),
     ]
     for c in own:
         c.start()
@@ -714,7 +718,7 @@
                 ).start()
 
     greet(place, False, owners)
-    for a in range(3):
+    for a in range(1):
         for kind in (XS, YS, S0):
             passing(a, kind).start()
     gup_s[...] = jnp.zeros_like(gup_s)
@@ -735,34 +739,34 @@
                 c.wait()
             router_copy.wait()
             router_s[...] = dot_nn(router_in[...], order_ref[...]).astype(BF)
-            for a in range(3):
+            for a in range(1):
                 got(a, S0)
             pltpu.make_async_copy(w_s, w_s, wsem.at[0]).wait()
 
         @pl.when(t == 1)
         def _():
-            for a in range(3):
+            for a in range(1):
                 got(a, XS)
                 passing(a, FA).start()
                 passing(a, S1).start()
                 got(a, YS)
                 passing(a, FB).start()
                 passing(a, S2).start()
-            for a in range(3):
+            for a in range(1):
                 got(a, S1)
 
         @pl.when(t == 2)
         def _():
-            for a in range(3):
+            for a in range(1):
                 got(a, FA)
                 got(a, FB)
                 passing(a, S3).start()
-            for a in range(3):
+            for a in range(1):
                 got(a, S2)
 
         @pl.when(t == 3)
         def _():
-            for a in range(3):
+            for a in range(1):
                 got(a, S3)
 
         tx, ty = t % 2, t // 2
@@ -803,7 +807,7 @@
         @pl.when(t == 1)
         def _():
             with_sib(0)
-            for a in range(3):
+            for a in range(1):
                 passing(a, FA).wait_send()
                 passing(a, S1).wait_send()
 
@@ -812,7 +816,7 @@
             with_sib(1)
             for a in (0, 1):
                 hop(a, HX0).start()
-            for a in range(3):
+            for a in range(1):
                 passing(a, FB).wait_send()
                 passing(a, S2).wait_send()
 
@@ -821,7 +825,7 @@
             with_sib(2)
             for a in (0, 1):
                 hop(a, HY0).start()
-            for a in range(3):
+            for a in range(1):
                 passing(a, S3).wait_send()
 
         for n in range(D // 256):
@@ -844,16 +848,30 @@
             def _():
                 to_sib(1, k).start()
 
+        def last(a):
+            @pl.when(t == 3)
+            def _():
+                to_sib(a, 3).wait_recv()
+                add(a, mine[3], 0, count, [(sib_s, (a, 3))])
+                hop(a, HY1).start()
+                hop(a, HX1).start()
+
+        last(0)
         for n in range(D // 256):
             where = pl.ds(n * 256, 256)
             gup_s[where, :] += dot_nn(mt_s[where, :], dpre_s[...])
+        last(1)
+        for n in range(D // 256):
+            where = pl.ds(n * 256, 256)
             gdn_s[where, :] += dot_nn(gt_s[where, :], hg_s[...])
 
     for a in (0, 1):
-        to_sib(a, 3).wait_recv()
-        add(a, mine[3], 0, count, [(sib_s, (a, 3))])
-        hop(a, HY1).start()
-        hop(a, HX1).start()
+        hop(a, HY1).wait_recv()
+        add(a, place.xnb, 0, half, [(first_s, (a, 1))])
+        hop(a, HX2).start()
+        hop(a, HX1).wait_recv()
+        add(a, place.ynb, half, half, [(first_s, (a, 3))])
+        hop(a, HY2).start()
     w_s[0] = gup_s[...].astype(BF)
     w_s[1] = gdn_s[...].astype(BF)
 
@@ -868,13 +886,6 @@
                 ).start()
 
     grouter_out[...] = gr_s[...].astype(BF)
-    for a in (0, 1):
-        hop(a, HY1).wait_recv()
-        add(a, place.xnb, 0, half, [(first_s, (a, 1))])
-        hop(a, HX2).start()
-        hop(a, HX1).wait_recv()
-        add(a, place.ynb, half, half, [(first_s, (a, 3))])
-        hop(a, HY2).start()
     for a, out in ((0, drow_out), (1, moe_out)):
         hop(a, HY0).wait_recv()
         hop(a, HX2).wait_recv()
@@ -882,7 +893,7 @@
         hop(a, HX0).wait_recv()
         hop(a, HY2).wait_recv()
         add(a, place.e, half, half, [(first_s, (a, 2)), (second_s, (a, 1))], out)
-    for a in range(3):
+    for a in range(1):
         for kind in (XS, YS, S0):
             passing(a, kind).wait_send()
     for a in (0, 1):
@@ -931,8 +942,8 @@
             pltpu.VMEM((2, 4, count, D), BF),
             pltpu.VMEM((2, 4, count // 2, D), BF),
             pltpu.VMEM((2, 2, count // 2, D), BF),
-            dma((3, 8)),
-            dma((3, 8)),
+            dma((1, 8)),
+            dma((1, 8)),
             dma((2, 10)),
             dma((2, 10)),
             dma((4,)),
@@ -949,106 +960,267 @@
     )(middle, cots, member, weights, packed, order, mine)
 
 
-def picked_mask(picks, number):
-    return jnp.sum(
-        (picks[..., None] == jnp.arange(number, dtype=jnp.int32)).astype(F32), axis=-2
-    )
-
-
-def layer_normed(inputs, gain_row):
-    centred = inputs - jnp.mean(inputs, axis=-1, keepdims=True)
-    variance = jnp.mean(centred * centred, axis=-1, keepdims=True)
-    return centred * lax.rsqrt(variance + epsilon) * gain_row
-
-
-def head_gates(select, value_mask, out_mask):
-    row_count = value_mask.shape[0]
-    value_gate = jax.nn.sigmoid(select[:, : H * NV]).reshape(row_count, H, NV) * value_mask
-    out_gate = jax.nn.sigmoid(select[:, H * NV :]).reshape(row_count, H, NV) * out_mask
-    return (value_gate, out_gate)
-
-
-def dense_forward(tokens, live, lengths, picks, gain, qkv, select_w, heads):
+def forward_kernel(
+    wide,
+    lanes,
+    lengths_ref,
+    x_ref,
+    choice_ref,
+    w_ref,
+    heads_ref,
+    qk_ref,
+    vals_ref,
+    sig_ref,
+    mask_ref,
+    vlow_ref,
+    prob_ref,
+    attended_ref,
+    mixed_ref,
+    middle_ref,
+    mlow_ref,
+):
+    count = x_ref.shape[0]
+    seq = count // MB
+    xf = x_ref[...].astype(F32)
+    centred = xf - jnp.mean(xf, axis=1, keepdims=True)
+    variance = jnp.mean(centred * centred, axis=1, keepdims=True)
+    gain_row = w_ref[:, pl.ds(wide + lanes, 128)].astype(F32).T[SEL : SEL + 1, :]
+    normed = (centred * lax.rsqrt(variance + epsilon) * gain_row).astype(BF)
+    for n in range(QK // 512):
+        cols = pl.ds(n * 512, 512)
+        qk_ref[:, cols] = dot_nn(normed, w_ref[:, cols]).astype(BF)
+    sig = jax.nn.sigmoid(dot_nn(x_ref[...], w_ref[:, pl.ds(wide + lanes, 128)]))
+    row = lax.broadcasted_iota(jnp.int32, (count, 128), 0)
+    lane = lax.broadcasted_iota(jnp.int32, (count, 128), 1)
+    live = (row < lengths_ref[0, 0]).astype(F32)
+    for b in range(1, MB):
+        live = jnp.where(row < b * seq, live, (row < b * seq + lengths_ref[b, 0]).astype(F32))
+    mask = jnp.zeros((count, 128), F32)
+    top = choice_ref.shape[1] // H
+    for v in range(H * top):
+        picked = choice_ref[:, v : v + 1] + NV * (v // top)
+        mask = mask + (picked == lane).astype(F32) + (picked + H * NV == lane).astype(F32) * live
+    sig_ref[...] = sig
+    mask_ref[...] = mask
+    gates = sig * mask
+    for h in range(H):
+        vals = dot_nn(x_ref[...], w_ref[:, pl.ds(QK + h * NV * HD, NV * HD)])
+        vals_ref[:, pl.ds(h * NV * HD, NV * HD)] = vals
+        total = gates[:, h * NV : h * NV + 1] * vals[:, :HD]
+        for e in range(1, NV):
+            at = h * NV + e
+            total = total + gates[:, at : at + 1] * vals[:, e * HD : (e + 1) * HD]
+        vlow_ref[:, pl.ds(h * HD, HD)] = total.astype(BF)
+    at_i = lax.broadcasted_iota(jnp.int32, (seq, seq), 0)
+    at_j = lax.broadcasted_iota(jnp.int32, (seq, seq), 1)
+    for b in range(MB):
+        allowed = (at_j <= at_i) & (at_j < lengths_ref[b, 0])
+        here = pl.ds(b * seq, seq)
+        for h in range(H):
+            queries = qk_ref[here, pl.ds(h * HD, HD)]
+            keys_all = qk_ref[here, pl.ds((H + h) * HD, HD)]
+            scores = jnp.where(allowed, dot_nt(queries, keys_all) * HD ** (-0.5), -1e30)
+            expo = jnp.exp(scores - jnp.max(scores, axis=1, keepdims=True))
+            prob = expo / jnp.sum(expo, axis=1, keepdims=True)
+            prob_ref[b * H + h] = prob
+            attended_ref[here, pl.ds(h * HD, HD)] = dot_nn(
+                prob.astype(BF), vlow_ref[here, pl.ds(h * HD, HD)]
+            )
+    for h in range(H):
+        attended = attended_ref[:, pl.ds(h * HD, HD)]
+        for e in range(NV):
+            at = h * NV + e
+            gate = gates[:, H * NV + at : H * NV + at + 1]
+            mixed_ref[:, pl.ds(at * HD, HD)] = (gate * attended).astype(BF)
+    for n in range(D // 512):
+        cols = pl.ds(n * 512, 512)
+        middle = x_ref[:, cols].astype(F32) + dot_nn(mixed_ref[...], heads_ref[:, cols])
+        middle_ref[:, cols] = middle
+        mlow_ref[:, cols] = middle.astype(BF)
+
+
+def forward(lengths, tokens, choice, packed, heads, wide, lanes):
     count = tokens.shape[0]
     seq = count // MB
-    xf = tokens.astype(F32)
-    value_mask = picked_mask(picks, NV)
-    out_mask = value_mask * live[:, None, None]
-    normed, norm_back = jax.vjp(layer_normed, xf, gain.astype(F32))
-    normed_low = normed.astype(BF)
-    query_key = dot_nn(normed_low, qkv[:, :QK]).astype(BF)
-    values_all = dot_nn(tokens, qkv[:, QK:])
-    select = dot_nn(tokens, select_w)
-    (value_gate, out_gate), gate_back = jax.vjp(
-        lambda logits_in: head_gates(logits_in, value_mask, out_mask), select
+    vmem = pl.BlockSpec(memory_space=pltpu.VMEM)
+    shape = jax.ShapeDtypeStruct
+    return pl.pallas_call(
+        functools.partial(forward_kernel, wide, lanes),
+        in_specs=[pl.BlockSpec(memory_space=pltpu.SMEM)] + [vmem] * 4,
+        out_specs=[vmem] * 10,
+        out_shape=[
+            shape((count, QK), BF),
+            shape((count, VAL), F32),
+            shape((count, 128), F32),
+            shape((count, 128), F32),
+            shape((count, H * HD), BF),
+            shape((MB * H, seq, seq), F32),
+            shape((count, H * HD), F32),
+            shape((count, VAL), BF),
+            shape((count, D), F32),
+            shape((count, D), BF),
+        ],
+        compiler_params=pltpu.CompilerParams(vmem_limit_bytes=56 * 1024 * 1024),
+        cost_estimate=pl.CostEstimate(
+            flops=2 * count * D * (wide + VAL),
+            bytes_accessed=(wide + VAL) * D * 2 + count * D * 20,
+            transcendentals=count * seq * H,
+        ),
+    )(lengths, tokens, choice, packed, heads)
+
+
+def backward_kernel(
+    wide,
+    lanes,
+    x_ref,
+    cots_ref,
+    drow_ref,
+    moe_ref,
+    middle_ref,
+    qk_ref,
+    vals_ref,
+    sig_ref,
+    mask_ref,
+    vlow_ref,
+    prob_ref,
+    attended_ref,
+    mixed_ref,
+    grouter_ref,
+    w_ref,
+    heads_ref,
+    out_ref,
+    dx_ref,
+    gw_ref,
+    gheads_ref,
+    dvals_s,
+    dqk_s,
+):
+    count = x_ref.shape[0]
+    seq = count // MB
+    out_ref[...] = (middle_ref[...] + moe_ref[...]).astype(BF)
+    d_middle = cots_ref[...].astype(F32) + drow_ref[...]
+    d_branch = d_middle.astype(BF)
+    mask = mask_ref[...]
+    sig = sig_ref[...]
+    gates = sig * mask
+    lane = lax.broadcasted_iota(jnp.int32, (1, 128), 1)
+    d_gates = jnp.zeros((count, 128), F32)
+    width = NV * HD
+    for h in range(H):
+        where = pl.ds(h * width, width)
+        gheads_ref[where, :] = dot_tn(mixed_ref[:, where], d_branch).astype(BF)
+        d_mixed = dot_nt(d_branch, heads_ref[where, :])
+        attended = attended_ref[:, pl.ds(h * HD, HD)]
+        total = jnp.zeros((count, HD), F32)
+        for e in range(NV):
+            at = H * NV + h * NV + e
+            part = d_mixed[:, e * HD : (e + 1) * HD]
+            total = total + gates[:, at : at + 1] * part
+            d_one = jnp.sum(part * attended, axis=1, keepdims=True)
+            d_gates = d_gates + d_one * (lane == at).astype(F32)
+        d_attended = total.astype(BF)
+        d_values = []
+        for b in range(MB):
+            here = pl.ds(b * seq, seq)
+            rows = slice(b * seq, (b + 1) * seq)
+            prob = prob_ref[b * H + h]
+            values = vlow_ref[here, pl.ds(h * HD, HD)]
+            d_prob = dot_nt(d_attended[rows], values)
+            d_scores = (
+                prob * (d_prob - jnp.sum(prob * d_prob, axis=1, keepdims=True))
+            ).astype(BF)
+            d_values.append(dot_tn(prob.astype(BF), d_attended[rows]).astype(BF).astype(F32))
+            queries = qk_ref[here, pl.ds(h * HD, HD)]
+            keys_all = qk_ref[here, pl.ds((H + h) * HD, HD)]
+            dqk_s[here, pl.ds(h * HD, HD)] = (dot_nn(d_scores, keys_all) * HD ** (-0.5)).astype(BF)
+            dqk_s[here, pl.ds((H + h) * HD, HD)] = (
+                dot_tn(d_scores, queries) * HD ** (-0.5)
+            ).astype(BF)
+        d_value = jnp.concatenate(d_values, axis=0)
+        for e in range(NV):
+            at = h * NV + e
+            cols = pl.ds(at * HD, HD)
+            d_one = jnp.sum(d_value * vals_ref[:, cols], axis=1, keepdims=True)
+            d_gates = d_gates + d_one * (lane == at).astype(F32)
+            dvals_s[:, cols] = (gates[:, at : at + 1] * d_value).astype(BF)
+    d_select = (d_gates * mask * sig * (1.0 - sig)).astype(BF)
+    x_t = x_ref[...].T
+    for n in range(VAL // 512):
+        cols = pl.ds(n * 512, 512)
+        gw_ref[:, pl.ds(QK + n * 512, 512)] = dot_nn(x_t, dvals_s[:, cols]).astype(BF)
+    xf = x_ref[...].astype(F32)
+    centred = xf - jnp.mean(xf, axis=1, keepdims=True)
+    variance = jnp.mean(centred * centred, axis=1, keepdims=True)
+    rstd = lax.rsqrt(variance + epsilon)
+    unit = centred * rstd
+    gain_row = w_ref[:, pl.ds(wide + lanes, 128)].astype(F32).T[SEL : SEL + 1, :]
+    normed_t = (unit * gain_row).astype(BF).T
+    for n in range(QK // 512):
+        cols = pl.ds(n * 512, 512)
+        gw_ref[:, cols] = dot_nn(normed_t, dqk_s[:, cols]).astype(BF)
+    d_normed = dot_nt(dqk_s[...], w_ref[:, pl.ds(0, QK)])
+    grad_gain = jnp.sum(d_normed * unit, axis=0, keepdims=True)
+    small = dot_tn(d_select, x_ref[...])
+    which = lax.broadcasted_iota(jnp.int32, (128, 1), 0)
+    gw_ref[:, pl.ds(wide + lanes, 128)] = jnp.where(which == SEL, grad_gain, small).T.astype(BF)
+    gw_ref[:, pl.ds(wide, lanes)] = grouter_ref[...]
+    scaled = d_normed * gain_row
+    dx_ref[...] = (
+        d_middle
+        + (
+            scaled
+            - jnp.mean(scaled, axis=1, keepdims=True)
+            - unit * jnp.mean(scaled * unit, axis=1, keepdims=True)
+        )
+        * rstd
     )
-    values_split = values_all.reshape(count, H, NV, HD)
-    values_low = jnp.sum(value_gate[..., None] * values_split, axis=2).astype(BF)
-    values_seq = values_low.reshape(MB, seq, H, HD)
-    queries = query_key[:, : H * HD].reshape(MB, seq, H, HD)
-    keys_all = query_key[:, H * HD :].reshape(MB, seq, H, HD)
-    position = jnp.arange(seq, dtype=jnp.int32)
-    scores = jnp.einsum("bihd,bjhd->bhij", queries, keys_all, preferred_element_type=F32) * HD ** (
-        -0.5
+    for n in range(D // 256):
+        rows = pl.ds(n * 256, 256)
+        dx_ref[:, rows] += dot_nt(dvals_s[...], w_ref[rows, pl.ds(QK, VAL)]) + dot_nt(
+            d_select, w_ref[rows, pl.ds(wide + lanes, 128)]
+        )
+
+
+def backward(tokens, cots, drow, moe_sum, saved, grouter, packed, heads, wide, lanes):
+    count = tokens.shape[0]
+    qk, vals, sig, mask, vlow, prob, attended, mixed, middle = saved
+    vmem = pl.BlockSpec(memory_space=pltpu.VMEM)
+    shape = jax.ShapeDtypeStruct
+    return pl.pallas_call(
+        functools.partial(backward_kernel, wide, lanes),
+        in_specs=[vmem] * 16,
+        out_specs=[vmem] * 4,
+        out_shape=[
+            shape((count, D), BF),
+            shape((count, D), F32),
+            shape(packed.shape, BF),
+            shape(heads.shape, BF),
+        ],
+        scratch_shapes=[pltpu.VMEM((count, VAL), BF), pltpu.VMEM((count, QK), BF)],
+        compiler_params=pltpu.CompilerParams(vmem_limit_bytes=62 * 1024 * 1024),
+        cost_estimate=pl.CostEstimate(
+            flops=4 * count * D * (wide + VAL),
+            bytes_accessed=(wide + VAL) * D * 4 + count * D * 30,
+            transcendentals=0,
+        ),
+    )(
+        tokens,
+        cots,
+        drow,
+        moe_sum,
+        middle,
+        qk,
+        vals,
+        sig,
+        mask,
+        vlow,
+        prob,
+        attended,
+        mixed,
+        grouter,
+        packed,
+        heads,
     )
-    allowed = (position[None, :] <= position[:, None])[None] & (
-        position[None, None, :] < lengths[:, None, None]
-    )
-    masked = jnp.where(allowed[:, None], scores, -1e30)
-    expo = jnp.exp(masked - jnp.max(masked, axis=-1, keepdims=True))
-    attention = expo / jnp.sum(expo, axis=-1, keepdims=True)
-    attended = jnp.einsum(
-        "bhij,bjhd->bihd", attention.astype(BF), values_seq, preferred_element_type=F32
-    ).reshape(count, H, HD)
-    mixed_heads = (out_gate[..., None] * attended[:, :, None, :]).reshape(count, VAL).astype(BF)
-    middle = xf + dot_nn(mixed_heads, heads)
-
-    def backward(d_middle):
-        d_branch = d_middle.astype(BF)
-        grad_heads = dot_tn(mixed_heads, d_branch)
-        d_mixed = dot_nt(d_branch, heads).reshape(count, H, NV, HD)
-        d_attended = jnp.sum(out_gate[..., None] * d_mixed, axis=2).astype(BF)
-        d_out_gate = jnp.sum(d_mixed * attended[:, :, None, :], axis=-1)
-        d_att_seq = d_attended.reshape(MB, seq, H, HD)
-        d_attention = jnp.einsum(
-            "bihd,bjhd->bhij", d_att_seq, values_seq, preferred_element_type=F32
-        )
-        d_scores = (
-            attention * (d_attention - jnp.sum(attention * d_attention, axis=-1, keepdims=True))
-        ).astype(BF)
-        d_values = (
-            jnp.einsum(
-                "bhij,bihd->bjhd", attention.astype(BF), d_att_seq, preferred_element_type=F32
-            )
-            .astype(BF)
-            .reshape(count, H, HD)
-        )
-        d_queries = jnp.einsum(
-            "bhij,bjhd->bihd", d_scores, keys_all, preferred_element_type=F32
-        ) * HD ** (-0.5)
-        d_keys = jnp.einsum(
-            "bhij,bihd->bjhd", d_scores, queries, preferred_element_type=F32
-        ) * HD ** (-0.5)
-        d_query_key = jnp.concatenate(
-            [d_queries.reshape(count, H * HD), d_keys.reshape(count, H * HD)], axis=1
-        ).astype(BF)
-        d_value_gate = jnp.sum(d_values[:, :, None, :] * values_split, axis=-1)
-        d_values_all = (value_gate[..., None] * d_values[:, :, None, :]).reshape(count, VAL).astype(BF)
-        d_select = gate_back((d_value_gate, d_out_gate))[0].astype(BF)
-        grad_qk = dot_tn(normed_low, d_query_key)
-        grad_val = dot_tn(tokens, d_values_all)
-        grad_select = dot_tn(tokens, d_select)
-        d_normed = dot_nt(d_query_key, qkv[:, :QK])
-        d_norm_in, grad_gain = norm_back(d_normed)
-        d_tokens = (
-            d_middle
-            + d_norm_in
-            + dot_nt(d_values_all, qkv[:, QK:])
-            + dot_nt(d_select, select_w)
-        )
-        return d_tokens, grad_gain, grad_qk, grad_val, grad_select, grad_heads
-
-    return middle, backward
 
 
 def body(
@@ -1128,35 +1300,28 @@
     ).astype(BF)
 
     if own_kernels:
-        packed_all, heads = gather(
-            (packed, heads_low), (True, True), (own_rows // 2, 48), owners, group, 0
+        packed_all, heads, cots_all, member_all = gather(
+            (packed, heads_low, flat_cots, member),
+            (True, True, False, False),
+            (own_rows // 2, 48, count // 2, count // 2),
+            owners,
+            group,
+            0,
         )
     else:
         packed_all = lax.all_gather(packed, both, axis=0, tiled=True)
         heads = lax.all_gather(heads_low, both, axis=0, tiled=True)
-    qkv = packed_all[:, :wide]
-    select_w = packed_all[:, wide + lanes : wide + lanes + SEL]
-    gain = packed_all[:, wide + lanes + SEL]
-
-    middle, backward = dense_forward(
-        flat_tokens,
-        live,
-        lengths[:, 0],
-        head_choice.reshape(count, H, -1),
-        gain,
-        qkv,
-        select_w,
-        heads,
-    )
-    middle_low = middle.astype(BF)
+        cots_all, member_all = (
+            lax.all_gather(a, "expert", axis=0, tiled=True) for a in (flat_cots, member)
+        )
+    choice = head_choice.reshape(count, -1)
+    *saved, middle_low = forward(lengths, flat_tokens, choice, packed_all, heads, wide, lanes)
     if own_kernels:
         d_from_rows, moe_sum, expert_grads, grad_router = fused_experts(
-            middle_low, flat_cots, member, weights, packed_all, wide, order_mine, mine_sel, 1
+            middle_low, cots_all, member_all, weights, packed_all, wide, order_mine, mine_sel, 1
         )
     else:
-        rows_all, cots_all, member_all = (
-            lax.all_gather(a, "expert", axis=0, tiled=True) for a in (middle_low, flat_cots, member)
-        )
+        rows_all = lax.all_gather(middle_low, "expert", axis=0, tiled=True)
         side = weights.reshape(owners, 2, slots, share, F).transpose(0, 1, 3, 2, 4)
         moe_part, drow_part, expert_grads, grad_router = moe(
             rows_all,
@@ -1176,38 +1341,38 @@
     expert_sum = lax.psum_scatter(
         expert_grads.reshape(owners * 2 * slots, share, F), "dp", scatter_dimension=0, tiled=True
     ).astype(F32)
-    mixed = (middle + moe_sum).astype(BF)
-
-    d_middle = flat_cots.astype(F32) + d_from_rows
-    d_tokens, grad_gain, grad_qk, grad_val, grad_select, grad_heads = backward(d_middle)
-    small_grads = jnp.concatenate(
-        [
-            grad_router,
-            grad_select.astype(BF),
-            grad_gain.astype(BF)[:, None],
-            jnp.zeros((D, 127 - SEL), BF),
-        ],
-        axis=1,
+    mixed, d_tokens, grad_packed, grad_heads = backward(
+        flat_tokens,
+        flat_cots,
+        d_from_rows,
+        moe_sum,
+        saved,
+        grad_router,
+        packed_all,
+        heads,
+        wide,
+        lanes,
     )
-    dense_grads = (grad_qk.astype(BF), grad_val.astype(BF), small_grads, grad_heads.astype(BF))
     if own_kernels:
-        sums = scatter(
-            tuple(g.reshape(owners, 4, 2, -1, G, g.shape[1]) for g in dense_grads),
-            (True,) * 4,
-            (1,) * 4,
-            owners,
-            3,
+        packed_sum, heads_sum = (
+            total.reshape(-1, total.shape[2])
+            for total in scatter(
+                tuple(g.reshape(owners, 4, 2, -1, G, g.shape[1]) for g in (grad_packed, grad_heads)),
+                (True, True),
+                (1, 1),
+                owners,
+                3,
+            )
         )
-        qk_sum, val_sum, small_sum, heads_sum = (s.reshape(-1, s.shape[2]) for s in sums)
     else:
-        qk_sum, val_sum, small_sum, heads_sum = (
+        packed_sum, heads_sum = (
             lax.psum_scatter(g, both, scatter_dimension=0, tiled=True).astype(F32)
-            for g in dense_grads
+            for g in (grad_packed, grad_heads)
         )
-    qkv_sum = jnp.concatenate([qk_sum, val_sum], axis=1)
-    router_sum = small_sum[:, :experts]
-    select_sum = small_sum[:, lanes : lanes + SEL]
-    gain_sum = small_sum[:, lanes + SEL]
+    qkv_sum = packed_sum[:, :wide]
+    router_sum = packed_sum[:, wide : wide + experts]
+    select_sum = packed_sum[:, wide + lanes : wide + lanes + SEL]
+    gain_sum = packed_sum[:, wide + lanes + SEL]
     up_sum = expert_sum[:slots]
     down_sum = expert_sum[slots:]
 

time: 483 us -> 447 us (0.925)
  matrix products: 58.5 us -> 0.9 us
  Pallas kernels: 324 us -> 374 us
  other arithmetic: 54.8 us -> 24.8 us
  waiting for transfers between devices: 0.04 us -> 20.7 us
  local copies, waits for them, and re-layouts: 25.1 us -> 6.54 us
    pallas_call x0 -> x2, Pallas kernels: none -> 47.7 us  [the longest x1 32.2 us: backward(): pl.pallas_call(functools.partial(backward_kernel, wide, lanes), in_specs=...]
    dot_general x13 -> x0, matrix products: 38.3 us -> none  [the longest x4 18.4 us: dot_nt(): lax.dot_general(a, b, (((1,), (1,)), ((), ())), preferred_element_type=F32)]
    dot_general x5 -> x1, matrix products: 18.7 us -> 0.9 us  [dot_nn(): return jnp.dot(a, b, preferred_element_type=F32)]
    all_gather x1, waiting for transfers between devices: 0.01 us -> 14.6 us  [body(): weights = lax.all_gather(experts_low, 'dp', axis=0, tiled=False)]
    reduce_sum x1, other arithmetic: 15.5 us -> 2.19 us  [body(): jnp.sum((routes.reshape(count, TOPK)[..., None] == lane_ids).astype(F32),...]
    pallas_call x1, Pallas kernels: 90.7 us -> 102 us  [gather(): pl.pallas_call(functools.partial(gather_kernel, owners, group, lines, hal...]
    pallas_call x1, Pallas kernels: 150 us -> 139 us  [fused_experts(): pl.pallas_call(functools.partial(fused_kernel, owners, slots, wide, 256),...]
    reduce_sum x7 -> x0, other arithmetic: 11 us -> none  [the longest x1 4.61 us: backward(): d_value_gate = jnp.sum(d_values[:, :, None, :] * values_split, axis=-1)]
  transfers between devices with their start and end apart: 2 -> 2, of which waited for: 0 -> 2; matrix products, arithmetic and copies ran while one was open for 24% -> 4% of each run, Pallas kernels for 36% -> 53%
where the time goes in v3:
time: 447 us; the launch traced here: 442 us
  Pallas kernels  374 us (84%)
  other arithmetic  24.8 us (6%)
  waiting for transfers between devices  20.7 us (5%)
  between operations  14.7 us (3%)
  local copies, waits for them, and re-layouts  6.54 us (1%)
    pallas_call x1, Pallas kernels, fused_experts(): pl.pallas_call(functools.partial(fused_kernel, owners, slots, wide, 256),...  139 us
    pallas_call x1, Pallas kernels, gather(): pl.pallas_call(functools.partial(gather_kernel, owners, group, lines, hal...  102 us
    pallas_call x1, Pallas kernels, scatter(): pl.pallas_call(functools.partial(scatter_kernel, owners, lines, subs), ou...  84.9 us
    pallas_call x1, Pallas kernels, backward(): pl.pallas_call(functools.partial(backward_kernel, wide, lanes), in_specs=...  32.2 us
    pallas_call x1, Pallas kernels, forward(): pl.pallas_call(functools.partial(forward_kernel, wide, lanes), in_specs=[...  15.5 us
    all_gather x1, waiting for transfers between devices, body(): weights = lax.all_gather(experts_low, 'dp', axis=0, tiled=False)  14.6 us
    convert_element_type x6, other arithmetic, update_weight(): return (new_moment, new_average, new_weight, new_weight.astype(BF))  10.2 us
  transfers between devices with their start and end apart: 2, of which 2 were waited for; matrix products, arithmetic and copies ran while one was open for 4% of the time, Pallas kernels for 53%

profile of v3, /device:TPU:0, one launch (start us, length us, event | category | flops | bytes accessed | tf_op | source)
XLA Modules:
  0.0 441.6 jit_solution(17495289732702427886)
XLA Ops:
  7.3 1.6 convert_element_type.81
  9.2 1.3 pad_maximum_fusion
  11.1 0.6 copy.76.lengths_ref
  12.2 0.7 convert_element_type.75.refs_1_
  12.9 0.8 copy.77.choice_ref
  13.9 0.8 concatenate.6.refs_0_
  14.7 2.2 convert_reduce_fusion
  16.9 0.9 convolution_convert_fusion.refs_3_
  17.8 102.2 %shard_map.490 = (bf16[1024,3840]{1,0:T(8,128)(2,1)}, bf16[2560,1024]{1,0:T(8,128)(2,1)}, bf16[3072,1024]{1,0:T(8,128)(2,1)}, bf16[3072,128]{1,0:T(8,128)(2,1)}) custom-call(bf16[32,3840]{1,0:T(8,128)(2,1)} %concatenate.6.refs_0_, bf16[80,1024]{1,0:T(8,128)(2,1)} %convert_element_type.75.refs_1_, bf16[384,1024]{1,0:T(8,128)(2,1)} %bitcast.27, ...), custom_call_target="tpu_custom_call" | custom-call | tf_op jit(solution)/shard_map/pallas_call | solution.py:249
  120.1 0.7 fusion.7
  120.8 15.5 %shard_map.491 = (bf16[384,1024]{1,0:T(8,128)(2,1)}, f32[384,2560]{1,0:T(8,128)}, f32[384,128]{1,0:T(8,128)}, f32[384,128]{1,0:T(8,128)}, bf16[384,512]{1,0:T(8,...) custom-call(s32[2,1]{1,0:T(2,128)} %copy.76.lengths_ref, ...), custom_call_target="tpu_custom_call" | custom-call | flops 4831838208 | bytes 20447232 | tf_op jit(solution)/shard_map/pallas_call | solution.py:1047
  136.3 14.6 %all-gather.3.cloned.1.call-done = bf16[96,256,128]{2,1,0:T(8,128)(2,1)} async-done(((bf16[24,256,128]{2,1,0:T(8,128)(2,1)}), bf16[96,256,128]{2,1,0:T(8,128)(2,1)}) %all-gather.3.cloned.1.call-update) | async-done | bytes 6291472 | tf_op jit(solution)/shard_map/all_gather | solution.py:1284
  150.8 139.1 %shard_map.492 = (f32[384,1024]{1,0:T(8,128)}, f32[384,1024]{1,0:T(8,128)}, bf16[4,24,256,128]{3,2,1,0:T(8,128)(2,1)}, bf16[1024,128]{1,0:T(8,128)(2,1)}) custom-call(bf16[384,1024]{1,0:T(8,128)(2,1)} %get-tuple-element.56.refs_0_, bf16[3072,1024]{1,0:T(8,128)(2,1)} %get-tuple-element.57.refs_1_, bf16[3072,128]{1,0:T(8,128)(2,1)} %get-tuple-element.58.refs_2_, ...), custom_call_target="tpu_custom_call" | custom-call | flops 57982058496 | bytes 12582912 | tf_op jit(solution)/shard_map/pallas_call | solution.py:917
  289.9 32.2 %shard_map.493 = (bf16[384,1024]{1,0:T(8,128)(2,1)}, f32[384,1024]{1,0:T(8,128)}, bf16[1024,3840]{1,0:T(8,128)(2,1)}, bf16[2560,1024]{1,0:T(8,128)(2,1)}) custom-call(bf16[384,1024]{1,0:T(8,128)(2,1)} %bitcast.37, bf16[384,1024]{1,0:T(8,128)(2,1)} %bitcast.28, f32[384,1024]{1,0:T(8,128)} %get-tuple-element.59.drow_ref, ...), custom_call_target="tpu_custom_call" | custom-call | flops 9663676416 | bytes 36962304 | tf_op jit(solution)/shard_map/pallas_call | solution.py:1189
  322.3 84.9 %shard_map.494 = (f32[2,16,3840]{2,1,0:T(8,128)}, f32[5,16,1024]{2,1,0:T(8,128)}) custom-call(bf16[4,4,2,2,16,3840]{5,4,3,2,1,0:T(8,128)(2,1)} %bitcast.24, bf16[4,4,2,5,16,1024]{5,4,3,2,1,0:T(8,128)(2,1)} %bitcast.26), custom_call_target="tpu_custom_call" | custom-call | tf_op jit(solution)/shard_map/pallas_call | solution.py:461
  407.2 1.0 slice_reduce_fusion
  408.2 0.5 fusion.16
  409.3 1.3 fusion.14
  410.6 0.6 add_multiply_fusion.5
  411.2 1.3 fusion.13
  412.6 0.6 add_multiply_fusion.4
  413.2 1.9 fusion.11
  415.0 0.8 add_multiply_fusion.3
  415.8 1.0 fusion.15
  416.8 0.8 copy-done.7
  417.6 0.8 add_multiply_fusion.2
  418.4 6.2 %reduce-scatter.2.cloned.1.call-done = bf16[24,256,128]{2,1,0:T(8,128)(2,1)} async-done(((bf16[96,256,128]{2,1,0:T(8,128)(2,1)}), bf16[24,256,128]{2,1,0:T(8,128)(2,1)}) %reduce-scatter.2.cloned.1.call-update) | async-done | bytes 1572880 | tf_op jit(solution)/shard_map/reduce_scatter | solution.py:1341
  424.5 1.9 convert_element_type.90
  426.4 4.3 fusion.9
  430.7 1.3 add_multiply_fusion
  432.4 0.5 copy-done.4
  433.3 1.3 add_multiply_fusion.1
  (94 shorter events, 2.9 us)
Async XLA Ops:
  7.2 1.9 copy-start
  7.2 143.6 %all-gather.3.cloned.1.call-start = ((), (), s32[]{:S(2)}) async-start(), calls=%async_computation.2 | async-start | bytes 7864320 | tf_op jit(solution)/shard_map/all_gather | solution.py:1284
  10.5 3.2 copy-start.25
  10.5 3.3 copy-start.5
  10.6 4.1 copy-start.32
  10.6 413.9 %reduce-scatter.2.cloned.1.call-start = ((), (), s32[]{:S(2)}) async-start(), calls=%async_computation.1 | async-start | bytes 7864320 | tf_op jit(solution)/shard_map/reduce_scatter | solution.py:1341
  322.1 86.1 %copy-start.34 = (f32[32]{0:T(128)S(1)}, f32[32]{0:T(128)}, u32[]{:S(2)}) copy-start(f32[32]{0:T(128)} %param.33) | copy-start | bytes 388
  322.1 86.1 %copy-start.35 = (f32[32]{0:T(128)S(1)}, f32[32]{0:T(128)}, u32[]{:S(2)}) copy-start(f32[32]{0:T(128)} %param.34) | copy-start | bytes 388
  322.2 86.6 %copy-start.37 = (f32[32]{0:T(128)S(1)}, f32[32]{0:T(128)}, u32[]{:S(2)}) copy-start(f32[32]{0:T(128)} %param.35) | copy-start | bytes 388
  322.2 87.1 %copy-start.22 = (f32[32,40]{1,0:T(8,128)S(1)}, f32[32,40]{1,0:T(8,128)}, u32[]{:S(2)}) copy-start(f32[32,40]{1,0:T(8,128)} %param.39) | copy-start | bytes 15364
  322.2 87.1 %copy-start.29 = (f32[32,40]{1,0:T(8,128)S(1)}, f32[32,40]{1,0:T(8,128)}, u32[]{:S(2)}) copy-start(f32[32,40]{1,0:T(8,128)} %param.40) | copy-start | bytes 15364
  322.2 88.4 %copy-start.26 = (f32[32,40]{1,0:T(8,128)S(1)}, f32[32,40]{1,0:T(8,128)}, u32[]{:S(2)}) copy-start(f32[32,40]{1,0:T(8,128)} %param.41) | copy-start | bytes 15364
  322.2 89.0 %copy-start.24 = (f32[32,96]{1,0:T(8,128)S(1)}, f32[32,96]{1,0:T(8,128)}, u32[]{:S(2)}) copy-start(f32[32,96]{1,0:T(8,128)} %param.42) | copy-start | bytes 36868
  322.2 89.0 %copy-start.30 = (f32[32,96]{1,0:T(8,128)S(1)}, f32[32,96]{1,0:T(8,128)}, u32[]{:S(2)}) copy-start(f32[32,96]{1,0:T(8,128)} %param.43) | copy-start | bytes 36868
  322.2 90.3 %copy-start.27 = (f32[32,96]{1,0:T(8,128)S(1)}, f32[32,96]{1,0:T(8,128)}, u32[]{:S(2)}) copy-start(f32[32,96]{1,0:T(8,128)} %param.44) | copy-start | bytes 36868
  322.2 90.9 %copy-start.12 = (f32[80,1024]{1,0:T(8,128)S(1)}, f32[80,1024]{1,0:T(8,128)}, u32[]{:S(2)}) copy-start(f32[80,1024]{1,0:T(8,128)} %param.45) | copy-start | bytes 983044
  322.3 90.9 %copy-start.17 = (f32[80,1024]{1,0:T(8,128)S(1)}, f32[80,1024]{1,0:T(8,128)}, u32[]{:S(2)}) copy-start(f32[80,1024]{1,0:T(8,128)} %param.46) | copy-start | bytes 983044
  407.1 7.9 %copy-start.18 = (f32[80,1024]{1,0:T(8,128)S(1)}, f32[80,1024]{1,0:T(8,128)}, u32[]{:S(2)}) copy-start(f32[80,1024]{1,0:T(8,128)} %param.47) | copy-start | bytes 983044
  407.1 8.7 %copy-start.6 = (f32[32,3584]{1,0:T(8,128)S(1)}, f32[32,3584]{1,0:T(8,128)}, u32[]{:S(2)}) copy-start(f32[32,3584]{1,0:T(8,128)} %param.36) | copy-start | bytes 1376260
  407.2 8.6 %copy-start.14 = (f32[2,16,3840]{2,1,0:T(8,128)S(1)}, f32[2,16,3840]{2,1,0:T(8,128)}, u32[]{:S(2)}) copy-start(f32[2,16,3840]{2,1,0:T(8,128)} %get-tuple-element.75) | copy-start | bytes 1474564
  407.2 8.6 %copy-start.15 = (f32[32,3584]{1,0:T(8,128)S(1)}, f32[32,3584]{1,0:T(8,128)}, u32[]{:S(2)}) copy-start(f32[32,3584]{1,0:T(8,128)} %param.37) | copy-start | bytes 1376260
  408.7 8.0 %copy-start.36 = (f32[32]{0:T(128)}, f32[32]{0:T(128)S(1)}, u32[]{:S(2)}) copy-start(f32[32]{0:T(128)S(1)} %get-tuple-element.97) | copy-start | bytes 388
  410.6 6.2 %copy-start.19 = (f32[32,40]{1,0:T(8,128)}, f32[32,40]{1,0:T(8,128)S(1)}, u32[]{:S(2)}) copy-start(f32[32,40]{1,0:T(8,128)S(1)} %get-tuple-element.91) | copy-start | bytes 15364
  412.5 4.2 copy-start.20
  415.0 1.7 copy-start.13
  415.0 2.5 copy-start.16
  418.4 8.0 %copy-start.1 = (f32[12,256,128]{2,1,0:T(8,128)S(1)}, f32[12,256,128]{2,1,0:T(8,128)}, u32[]{:S(2)}) copy-start(f32[12,256,128]{2,1,0:T(8,128)} %param.51) | copy-start | bytes 4718596
  418.4 8.0 %copy-start.2 = (f32[12,256,128]{2,1,0:T(8,128)S(1)}, f32[12,256,128]{2,1,0:T(8,128)}, u32[]{:S(2)}) copy-start(f32[12,256,128]{2,1,0:T(8,128)} %param.48) | copy-start | bytes 4718596
  424.5 1.9 copy-start.8
  426.4 4.3 copy-start.9
  430.7 2.2 copy-start.4
  430.7 2.6 copy-start.10
  (8 other events, 11.0 us)
Sparse Core Ops, SparseCore 0:
  10.7 140.0 all-gather.2
  290.1 134.4 reduce-scatter.1
